TPU v7x, 128 devices: a whole 4x4x4 slice. The times are simulated.
128 devices in a mesh: fibre: 16 (over x, y_lo, core), freq: 8 (over z, y_hi).
Axes of the slice: x: 4, y: 4 (y_hi: 2, y_lo: 2; y = y_hi * 2 + y_lo), z: 4, core: 2. Of those that a mesh axis runs over, the one named last changes fastest.
Arguments:
- records: bfloat16 [48, 6000, 2048], P('freq', 'fibre'), may hold values from -6 to 6
- channel_live: int32 [2048], P('fibre'), may hold values 0 or 1
- offset_limit: int32 [2048], P('fibre'), may hold values from 1 to 64
Outputs:
- stacked: float32 [64, 2, 512, 2048], P(None, None, 'freq', 'fibre')
All inputs are finite; a program needn't handle non-finite values. No bound on the sum of `channel_live` on one device may be relied on, other than what follows from the above.
Results may differ from a plain program's by a relative error of at most 0.0055.
Values may be sent and summed in bfloat16 or wider, within the bound.
No kernel may reach another device: no remote copies, remote signals or barrier semaphores. Data moves between devices by JAX's collectives and lax.ppermute only.
A program may use at most 128 MiB of HBM per device.

v0:
```python
import math

import jax
import jax.numpy as jnp
from jax import lax
from jax.sharding import PartitionSpec as P

SAMPLES = 6000
NB = 512
HALF = 32
FIRST_BIN = 60
OFFSETS = 64


def passed_along(value, axis, by):
    devices = lax.axis_size(axis)
    pairs = [(i, i + by) for i in range(devices) if 0 <= i + by < devices]
    return lax.ppermute(value, axis, pairs)


def make_table(samples, first, count):
    steps = lax.iota(jnp.int32, samples)[:, None]
    bins = first + lax.iota(jnp.int32, count)[None, :]
    phase = (steps * bins % samples).astype(jnp.float32) * (2.0 * math.pi / samples)
    taper = 0.5 - 0.5 * jnp.cos(steps.astype(jnp.float32) * (2.0 * math.pi / samples))
    return jnp.concatenate([taper * jnp.cos(phase), -taper * jnp.sin(phase)], axis=1).astype(
        jnp.bfloat16
    )


def whiten(spectra, live, kept, margin):
    extent = kept + 2 * margin
    real_part = spectra[:, :extent]
    imag_part = spectra[:, extent:]
    amplitude = jnp.sqrt(real_part * real_part + imag_part * imag_part)
    rows = lax.iota(jnp.int32, kept)[:, None]
    cols = lax.iota(jnp.int32, extent)[None, :]
    band = jnp.where(
        (cols >= rows) & (cols <= rows + 2 * margin), 1.0 / (2 * margin + 1), 0.0
    ).astype(jnp.float32)
    smooth = jnp.einsum("bj,wjc->wbc", band, amplitude, precision=lax.Precision.HIGHEST)
    scale = live[None, None, :] / (smooth + 1e-06)
    white = jnp.stack(
        [
            real_part[:, margin : margin + kept] * scale,
            imag_part[:, margin : margin + kept] * scale,
        ],
        axis=1,
    )
    return white.astype(jnp.bfloat16)


def cross_spectra(local, extended, count):
    width = local.shape[3]
    group = 8
    first_re = local[:, 0].astype(jnp.float32)
    first_im = local[:, 1].astype(jnp.float32)

    def one_group(start):
        window = lax.dynamic_slice_in_dim(extended, start + 1, width + group - 1, 3)
        results = []
        for inner in range(group):
            partner = window[:, :, :, inner : inner + width]
            second_re = partner[:, 0].astype(jnp.float32)
            second_im = partner[:, 1].astype(jnp.float32)
            real_sum = jnp.sum(first_re * second_re + first_im * second_im, axis=0)
            imag_sum = jnp.sum(first_im * second_re - first_re * second_im, axis=0)
            results.append(jnp.stack([real_sum, imag_sum], axis=0))
        return jnp.stack(results, axis=0)

    starts = lax.iota(jnp.int32, count // group) * group
    blocks = lax.map(one_group, starts)
    return blocks.reshape((count,) + blocks.shape[2:])


def body(records, channel_live, offset_limit):
    table = make_table(SAMPLES, FIRST_BIN, NB + 2 * HALF)
    live = channel_live.astype(jnp.float32)
    channel_block = lax.all_to_all(records, "fibre", split_axis=2, concat_axis=1, tiled=True)
    spectra = jnp.einsum("sj,wsc->wjc", table, channel_block, preferred_element_type=jnp.float32)
    white = whiten(spectra, live, NB, HALF)
    spectra_all = lax.all_to_all(white, "freq", split_axis=2, concat_axis=0, tiled=True)
    rim_part = spectra_all[:, :, :, :OFFSETS]
    above = passed_along(rim_part, "fibre", -1)
    extended = jnp.concatenate([spectra_all, above], axis=3)
    cross = cross_spectra(spectra_all, extended, OFFSETS)
    keep = (lax.iota(jnp.int32, OFFSETS)[:, None] + 1 <= offset_limit[None, :]).astype(jnp.float32)
    return cross * keep[:, None, None, :]


def solution(mesh):
    return jax.shard_map(
        body,
        mesh=mesh,
        in_specs=(P("freq", "fibre", None), P("fibre"), P("fibre")),
        out_specs=P(None, None, "freq", "fibre"),
        check_vma=False,
    )
```

profile of v0, /device:TPU:1, one launch (start us, length us, event | category | flops | bytes accessed | tf_op | source)
XLA Modules:
  0.0 442.9 jit_solution(8209929751714772166)
XLA Ops:
  0.0 15.8 %copy.22 = bf16[6,375,2048]{1,0,2:T(8,128)(2,1)} copy(bf16[6,375,2048]{2,1,0:T(8,128)(2,1)} %param.5) | data formatting | bytes 18432000 | tf_op args[0]
  15.8 0.0 copy-start.1
  15.8 7.0 %all-to-all-start = ((bf16[6,375,2048]{1,0,2:T(8,128)(2,1)}), bf16[6,375,2048]{1,0,2:T(8,128)(2,1)}, u32[]{:S(2)}, u32[]{:S(2)}) async-start(bf16[6,375,2048]{1,0,2:T(8,128)(2,1)} %copy.22), calls=%async_computation | async-start | bytes 25165824 | tf_op jit(solution)/shard_map/all_to_all | solution.py:79
  22.8 0.0 copy-done.1
  22.8 0.1 multiply_subtract_fusion
  22.9 67.3 %multiply_convert_fusion.1 = (bf16[6000,576]{1,0:T(8,128)(2,1)}, bf16[6000,576]{1,0:T(8,128)(2,1)}) fusion(s32[576]{0:T(1024)S(1)} %iota_add_fusion, f32[6000]{0:T(1024)S(1)} %get-tuple-element.141, f32[6000]{0:T(1024)S(1)} %get-tuple-element.142), kind=kLoop, calls=%fused_computation.101 | loop fusion | flops 44928000 | bytes 13874304 | tf_op jit(solution)/shard_map/convert.22
  90.2 132.8 %all-to-all-done = bf16[6,375,2048]{1,0,2:T(8,128)(2,1)} async-done(((bf16[6,375,2048]{1,0,2:T(8,128)(2,1)}), bf16[6,375,2048]{1,0,2:T(8,128)(2,1)}, u32[]{:S(2)}, u32[]{:S(2)}) %all-to-all-start) | async-done | bytes 9216032 | tf_op jit(solution)/shard_map/all_to_all | solution.py:79
  223.0 15.3 %copy.23 = bf16[6,375,16,128]{3,1,2,0:T(8,128)(2,1)} copy(bf16[6,375,16,128]{1,0,3,2:T(8,128)(2,1)} %bitcast.60) | data formatting | bytes 18432000 | tf_op jit(solution)/shard_map/all_to_all | solution.py:79
  238.3 12.3 %all_to_all.29 = bf16[6,6000,128]{2,1,0:T(8,128)(2,1)} reshape(bf16[6,16,375,128]{3,2,1,0:T(8,128)(2,1)} %bitcast.265) | data formatting | bytes 18432000 | tf_op jit(solution)/shard_map/all_to_all | solution.py:79
  250.6 19.2 %fusion.48 = f32[6,1152,128]{2,1,0:T(8,128)S(1)} fusion(bf16[6,6000,128]{2,1,0:T(8,128)(2,1)} %all_to_all.29, bf16[6000,576]{1,0:T(8,128)(2,1)} %get-tuple-element.140, bf16[6000,576]{1,0:T(8,128)(2,1)} %get-tuple-element.139), kind=kOutput, calls=%fused_computation.111 | convolution fusion | flops 10644480000 | bytes 26578944 | tf_op jit(solution)/shard_map/sj,wsc->wjc/dot_general | solution.py:80
  269.8 4.7 %fusion.61 = (bf16[6,1,512,128]{3,2,0,1:T(8,128)(2,1)S(1)}, bf16[6,1,512,128]{3,2,0,1:T(8,128)(2,1)S(1)}) fusion(f32[6,1152,128]{2,1,0:T(8,128)S(1)} %fusion.48, s32[512]{0:T(512)S(1)} %iota_add_fusion.1, f32[128]{0:T(128)S(1)} %convert_element_type.188), kind=kOutput, calls=%fused_computation.129 | convolution fusion | flops 2722775040 | bytes 8260096 | tf_op jit(solution)/shard_map/bj,wjc->wbc/dot_general | solution.py:41
  274.6 0.1 pad_maximum_fusion.1
  274.7 1.6 copy.25
  276.3 46.0 %all_to_all.36 = bf16[6,2,512,128]{3,1,0,2:T(2,128)(2,1)S(1)} all-to-all(bf16[6,2,512,128]{3,1,0,2:T(2,128)(2,1)S(1)} %copy.25), channel_id=1, replica_groups=mesh['fibre'=16,'freq'=8] {'freq'}, dimensions={2} | all-to-all | bytes 3145728 | tf_op jit(solution)/shard_map/all_to_all | solution.py:82
  322.3 0.4 copy.26
  322.7 3.7 collective-permute-start
  326.5 0.0 copy-done
  326.5 0.1 compare_convert_fusion
  326.6 2.1 fusion.63
  328.7 15.8 %collective-permute-done = bf16[48,2,64,64]{3,2,0,1:T(8,128)(2,1)S(1)} collective-permute-done((bf16[48,2,64,64]{3,2,0,1:T(8,128)(2,1)S(1)}, bf16[48,2,64,64]{3,2,0,1:T(8,128)(2,1)S(1)}, u32[]{:S(2)}, u32[]{:S(2)}) %collective-permute-start) | collective-permute-done | bytes 786464 | tf_op jit(solution)/shard_map/ppermute | solution.py:18
  344.5 1.1 pad_maximum_fusion
  345.6 0.2 copy.27
  345.8 91.9 %while.12 = (s32[]{:T(128)}, f32[8,8,2,64,128]{4,3,2,1,0:T(8,128)}, s32[8]{0:T(128)S(1)}, bf16[48,2,64,192]{3,2,1,0:T(8,128)(2,1)S(1)}, f32[48,64,128]{2,1,0:T(8...) while((s32[]{:T(128)}, f32[8,8,2,64,128]{4,3,2,1,0:T(8,128)}, ...), condition=%wide.region_17.18_spmd, body=%wide.region_0.17_spmd.sunk | while | flops 31457292 | bytes 18350440 | solution.py:72
  345.8 0.6 dynamic_slice.14
  347.7 8.6 %fusion.89 = (f32[64,128]{1,0:T(8,128)S(1)}, f32[64,128]{1,0:T(8,128)S(1)}, f32[64,128]{1,0:T(8,128)S(1)}, f32[64,128]{1,0:T(8,128)S(1)}, f32[64,128]{1,0:T(8,12...) fusion(f32[48,64,128]{2,1,0:T(8,128)} %get-tuple-element.250, ...), kind=kLoop, calls=%fused_computation.61.clone.1 | loop fusion | flops 31326208 | bytes 16252964 | tf_op jit(solution)/shard_map/while/body/eval_jaxpr/reduce_sum | solution.py:66
  356.5 0.8 bitcast_dynamic-update-slice_fusion.2
  357.3 0.6 dynamic_slice.14
  359.2 8.6 %fusion.89 = (f32[64,128]{1,0:T(8,128)S(1)}, f32[64,128]{1,0:T(8,128)S(1)}, f32[64,128]{1,0:T(8,128)S(1)}, f32[64,128]{1,0:T(8,128)S(1)}, f32[64,128]{1,0:T(8,12...) fusion(f32[48,64,128]{2,1,0:T(8,128)} %get-tuple-element.250, ...), kind=kLoop, calls=%fused_computation.61.clone.1 | loop fusion | flops 31326208 | bytes 16252964 | tf_op jit(solution)/shard_map/while/body/eval_jaxpr/reduce_sum | solution.py:66
  367.9 0.9 bitcast_dynamic-update-slice_fusion.2
  368.8 0.6 dynamic_slice.14
  370.7 8.6 %fusion.89 = (f32[64,128]{1,0:T(8,128)S(1)}, f32[64,128]{1,0:T(8,128)S(1)}, f32[64,128]{1,0:T(8,128)S(1)}, f32[64,128]{1,0:T(8,128)S(1)}, f32[64,128]{1,0:T(8,12...) fusion(f32[48,64,128]{2,1,0:T(8,128)} %get-tuple-element.250, ...), kind=kLoop, calls=%fused_computation.61.clone.1 | loop fusion | flops 31326208 | bytes 16252964 | tf_op jit(solution)/shard_map/while/body/eval_jaxpr/reduce_sum | solution.py:66
  379.4 0.9 bitcast_dynamic-update-slice_fusion.2
  380.3 0.6 dynamic_slice.14
  382.2 8.6 %fusion.89 = (f32[64,128]{1,0:T(8,128)S(1)}, f32[64,128]{1,0:T(8,128)S(1)}, f32[64,128]{1,0:T(8,128)S(1)}, f32[64,128]{1,0:T(8,128)S(1)}, f32[64,128]{1,0:T(8,12...) fusion(f32[48,64,128]{2,1,0:T(8,128)} %get-tuple-element.250, ...), kind=kLoop, calls=%fused_computation.61.clone.1 | loop fusion | flops 31326208 | bytes 16252964 | tf_op jit(solution)/shard_map/while/body/eval_jaxpr/reduce_sum | solution.py:66
  390.9 0.9 bitcast_dynamic-update-slice_fusion.2
  391.8 0.6 dynamic_slice.14
  393.6 8.6 %fusion.89 = (f32[64,128]{1,0:T(8,128)S(1)}, f32[64,128]{1,0:T(8,128)S(1)}, f32[64,128]{1,0:T(8,128)S(1)}, f32[64,128]{1,0:T(8,128)S(1)}, f32[64,128]{1,0:T(8,12...) fusion(f32[48,64,128]{2,1,0:T(8,128)} %get-tuple-element.250, ...), kind=kLoop, calls=%fused_computation.61.clone.1 | loop fusion | flops 31326208 | bytes 16252964 | tf_op jit(solution)/shard_map/while/body/eval_jaxpr/reduce_sum | solution.py:66
  402.4 0.8 bitcast_dynamic-update-slice_fusion.2
  403.2 0.6 dynamic_slice.14
  405.1 8.6 %fusion.89 = (f32[64,128]{1,0:T(8,128)S(1)}, f32[64,128]{1,0:T(8,128)S(1)}, f32[64,128]{1,0:T(8,128)S(1)}, f32[64,128]{1,0:T(8,128)S(1)}, f32[64,128]{1,0:T(8,12...) fusion(f32[48,64,128]{2,1,0:T(8,128)} %get-tuple-element.250, ...), kind=kLoop, calls=%fused_computation.61.clone.1 | loop fusion | flops 31326208 | bytes 16252964 | tf_op jit(solution)/shard_map/while/body/eval_jaxpr/reduce_sum | solution.py:66
  413.9 0.9 bitcast_dynamic-update-slice_fusion.2
  414.7 0.6 dynamic_slice.14
  416.6 8.6 %fusion.89 = (f32[64,128]{1,0:T(8,128)S(1)}, f32[64,128]{1,0:T(8,128)S(1)}, f32[64,128]{1,0:T(8,128)S(1)}, f32[64,128]{1,0:T(8,128)S(1)}, f32[64,128]{1,0:T(8,12...) fusion(f32[48,64,128]{2,1,0:T(8,128)} %get-tuple-element.250, ...), kind=kLoop, calls=%fused_computation.61.clone.1 | loop fusion | flops 31326208 | bytes 16252964 | tf_op jit(solution)/shard_map/while/body/eval_jaxpr/reduce_sum | solution.py:66
  425.4 0.8 bitcast_dynamic-update-slice_fusion.2
  426.2 0.6 dynamic_slice.14
  428.1 8.6 %fusion.89 = (f32[64,128]{1,0:T(8,128)S(1)}, f32[64,128]{1,0:T(8,128)S(1)}, f32[64,128]{1,0:T(8,128)S(1)}, f32[64,128]{1,0:T(8,128)S(1)}, f32[64,128]{1,0:T(8,12...) fusion(f32[48,64,128]{2,1,0:T(8,128)} %get-tuple-element.250, ...), kind=kLoop, calls=%fused_computation.61.clone.1 | loop fusion | flops 31326208 | bytes 16252964 | tf_op jit(solution)/shard_map/while/body/eval_jaxpr/reduce_sum | solution.py:66
  436.8 0.9 bitcast_dynamic-update-slice_fusion.2
  437.7 5.2 %bitcast_multiply_fusion = f32[64,2,64,128]{3,2,1,0:T(8,128)} fusion(f32[8,8,2,64,128]{4,3,2,1,0:T(8,128)} %get-tuple-element.82, f32[64,128]{1,0:T(8,128)S(1)} %compare_convert_fusion), kind=kLoop, calls=%fused_computation.110 | loop fusion | flops 1048576 | bytes 8421376 | tf_op jit(solution)/shard_map/mul | solution.py:88
  (71 shorter events, 0.5 us)
Async XLA Ops:
  15.8 7.0 %copy-start.1 = (s32[128]{0:T(128)S(1)}, s32[128]{0:T(128)}, u32[]{:S(2)}) copy-start(s32[128]{0:T(128)} %param.6) | copy-start | bytes 1540
  15.8 207.1 %all-to-all-start = ((bf16[6,375,2048]{1,0,2:T(8,128)(2,1)}), bf16[6,375,2048]{1,0,2:T(8,128)(2,1)}, u32[]{:S(2)}, u32[]{:S(2)}) async-start(bf16[6,375,2048]{1,0,2:T(8,128)(2,1)} %copy.22), calls=%async_computation | async-start | bytes 25165824 | tf_op jit(solution)/shard_map/all_to_all | solution.py:79
  322.3 4.2 copy-start
  322.7 21.7 %collective-permute-start = (bf16[48,2,64,64]{3,2,0,1:T(8,128)(2,1)S(1)}, bf16[48,2,64,64]{3,2,0,1:T(8,128)(2,1)S(1)}, u32[]{:S(2)}, u32[]{:S(2)}) collective-permute-start(bf16[48,2,64,64]{3,2,0,1:T(8,128)(2,1)S(1)} %bitcast.266), channel_id=1, source_target_pairs={{8,0},{16,8},{24,16},{32,24},{40,32},{48,40},{56,48},{64,56},{72,6... | collective-permute-start | bytes 2359304 | tf_op jit(solution)/shard_map/ppermute | solution.py:18
where the time goes:
time: 444 us; the launch traced here: 443 us
  waiting for transfers between devices  149 us (34%)
  other arithmetic  145 us (33%)
  local copies, waits for them, and re-layouts  57.6 us (13%)
  blocking collectives  46 us (10%)
  matrix products  23.9 us (5%)
  starting transfers between devices  10.7 us (2%)
  loops' own time  10.6 us (2%)
    all_to_all x1, waiting for transfers between devices, body(): lax.all_to_all(records, 'fibre', split_axis=2, concat_axis=1, tiled=True)  133 us
    reduce_sum x8, other arithmetic, one_group(): real_sum = jnp.sum(first_re * second_re + first_im * second_im, axis=0)  68.9 us
    another operation x1, other arithmetic  67.3 us
    all_to_all x1, blocking collectives, body(): lax.all_to_all(white, 'freq', split_axis=2, concat_axis=0, tiled=True)  46 us
    all_to_all x2, local copies, waits for them, and re-layouts, body(): lax.all_to_all(records, 'fibre', split_axis=2, concat_axis=1, tiled=True)  27.6 us
    dot_general x1, matrix products, body(): jnp.einsum('sj,wsc->wjc', table, channel_block, preferred_element_type=jn...  19.2 us
    unnamed x5, local copies, waits for them, and re-layouts  15.8 us
    ppermute x1, waiting for transfers between devices, passed_along(): return lax.ppermute(value, axis, pairs)  15.8 us
  transfers between devices with their start and end apart: 2, of which 2 were waited for; matrix products, arithmetic and copies ran while one was open for 16% of the time, Pallas kernels for 0%

commit v1 on v0

v1 whole, which is shorter than its diff:
```python
import functools

import jax
import jax.numpy as jnp
import numpy as np
from jax import lax
from jax.experimental import pallas as pl
from jax.experimental.pallas import tpu as pltpu
from jax.sharding import PartitionSpec as P

SAMPLES = 6000
NB = 512
HALF = 32
FIRST_BIN = 60
OFFSETS = 64
BINS = NB + 2 * HALF
RANK = 96
LANES = 128
F32 = jnp.float32
BF16 = jnp.bfloat16


def split_pair(values):
    high = values.astype(jnp.bfloat16)
    low = (values - high.astype(np.float64)).astype(jnp.bfloat16)
    return high, low


def make_tables(parts):
    run = SAMPLES // parts
    times = np.arange(run) - (run - 1) / 2
    bins = np.arange(FIRST_BIN - 1, FIRST_BIN + BINS + 1)
    weight = 1.0 + np.arange(len(bins)) / len(bins)
    angles = 2.0 * np.pi * np.outer(times, bins) / SAMPLES
    rows = []
    for wave in (np.cos, np.sin):
        vectors = np.linalg.svd(wave(angles) * weight, full_matrices=False)[0]
        vectors = vectors[:, : RANK // 2]
        rows.append((vectors * np.sign(vectors[run // 2 + 3])).T)
    down = np.concatenate(rows)
    samples = np.arange(SAMPLES)
    kept = np.arange(FIRST_BIN, FIRST_BIN + BINS)
    taper = 0.5 - 0.5 * np.cos(2.0 * np.pi * samples / SAMPLES)
    phase = 2.0 * np.pi * (np.outer(samples, kept) % SAMPLES) / SAMPLES
    table = np.concatenate([np.cos(phase), -np.sin(phase)], axis=1) * taper[:, None]
    back = np.einsum("psj,rs->jpr", table.reshape(parts, run, 2 * BINS), down)
    return down, back.reshape(2 * BINS, parts * RANK)


def project_kernel(down_ref, records_ref, out_ref):
    parts = out_ref.shape[0]
    wide = 4
    for start in range(0, parts, wide):
        block = records_ref[0, :, start * LANES : (start + wide) * LANES]
        both = jnp.dot(down_ref[...], block, preferred_element_type=F32)
        sums = (both[:RANK] + both[RANK:]).astype(BF16)
        for part in range(wide):
            out_ref[start + part, 0] = sums[:, part * LANES : (part + 1) * LANES]


def project(down, records, parts):
    windows, run, channels = records.shape
    return pl.pallas_call(
        project_kernel,
        grid=(windows,),
        in_specs=[
            pl.BlockSpec((2 * RANK, run), lambda w: (0, 0)),
            pl.BlockSpec((1, run, channels), lambda w: (w, 0, 0)),
        ],
        out_specs=pl.BlockSpec((parts, 1, RANK, LANES), lambda w: (0, w, 0, 0)),
        out_shape=jax.ShapeDtypeStruct((parts, windows, RANK, LANES), BF16),
        compiler_params=pltpu.CompilerParams(vmem_limit_bytes=40 * 2**20),
        cost_estimate=pl.CostEstimate(
            flops=4 * RANK * run * channels * windows,
            bytes_accessed=2 * records.size + 2 * parts * windows * RANK * LANES,
            transcendentals=0,
        ),
        name="project",
    )(down, records)


def up_by(values, rows):
    return pltpu.roll(values, values.shape[0] - rows, axis=0)


def whiten_kernel(live_ref, back_ref, sums_ref, first_ref, second_ref):
    parts = sums_ref.shape[0]
    columns = jnp.concatenate(
        [sums_ref[:, i].reshape(parts * RANK, LANES) for i in range(2)], axis=1
    )
    spectra = jnp.dot(back_ref[...], columns, preferred_element_type=F32)
    real_part = spectra[:BINS]
    imag_part = spectra[BINS:]
    amplitude = jnp.sqrt(real_part * real_part + imag_part * imag_part)
    total = amplitude
    for reach in (1, 2, 4):
        total = total + up_by(total, reach)
    for reach in (8, 16, 32):
        total = total[: total.shape[0] - reach] + total[reach:]
    smooth = (total[:NB] + amplitude[2 * HALF :]) * (1.0 / (2 * HALF + 1))
    live = live_ref[...].astype(F32)
    scale = jnp.concatenate([live, live], axis=1) / (smooth + 1e-06)
    real_part = real_part[HALF : HALF + NB] * scale
    imag_part = imag_part[HALF : HALF + NB] * scale
    groups = first_ref.shape[0]
    left = lax.broadcasted_iota(jnp.int32, (NB, LANES), 1) < LANES // 2
    for i in range(2):
        real_one = real_part[:, i * LANES : (i + 1) * LANES]
        imag_one = imag_part[:, i * LANES : (i + 1) * LANES]
        first = jnp.where(left, real_one, pltpu.roll(imag_one, LANES // 2, axis=1))
        second = jnp.where(left, pltpu.roll(real_one, LANES // 2, axis=1), imag_one)
        first_ref[:, i] = first.astype(BF16).reshape(groups, NB // groups, LANES)
        second_ref[:, i] = second.astype(BF16).reshape(groups, NB // groups, LANES)


def whiten(live, back, sums, groups):
    parts, windows = sums.shape[:2]
    shape = (groups, windows, NB // groups, LANES)
    half = pl.BlockSpec((groups, 2, NB // groups, LANES), lambda w: (0, w, 0, 0))
    return pl.pallas_call(
        whiten_kernel,
        grid=(windows // 2,),
        in_specs=[
            pl.BlockSpec((1, LANES), lambda w: (0, 0)),
            pl.BlockSpec(back.shape, lambda w: (0, 0)),
            pl.BlockSpec((parts, 2, RANK, LANES), lambda w: (0, w, 0, 0)),
        ],
        out_specs=[half, half],
        out_shape=[jax.ShapeDtypeStruct(shape, BF16)] * 2,
        compiler_params=pltpu.CompilerParams(vmem_limit_bytes=48 * 2**20),
        cost_estimate=pl.CostEstimate(
            flops=2 * back.size * windows * LANES,
            bytes_accessed=2 * (back.size + sums.size + 2 * windows * NB * LANES),
            transcendentals=0,
        ),
        name="whiten",
    )(live, back, sums)


def cross_kernel(limit_ref, first_ref, second_ref, next_ref, out_ref, real_own, imag_own, real_next, imag_next):
    groups, windows, bins, _ = first_ref.shape
    every = groups * windows
    half = LANES // 2
    left = lax.broadcasted_iota(jnp.int32, (every * bins, LANES), 1) < half
    first = first_ref[...].astype(F32).reshape(every * bins, LANES)
    second = second_ref[...].astype(F32).reshape(every * bins, LANES)
    real_own[...] = jnp.where(left, first, pltpu.roll(second, half, axis=1))
    imag_own[...] = jnp.where(left, pltpu.roll(first, half, axis=1), second)
    after = next_ref[...].astype(F32).reshape(every * bins, LANES)
    real_next[...] = after
    imag_next[...] = pltpu.roll(after, half, axis=1)
    offsets = lax.broadcasted_iota(jnp.int32, (OFFSETS, LANES), 0) + 1
    keep = (offsets <= limit_ref[...]).astype(F32)
    lane = lax.broadcasted_iota(jnp.int32, (LANES, LANES), 1)

    def skewed(gram):
        for bit in (64, 32, 16, 8):
            rows = gram.shape[0] - bit
            if bit == 64:
                rows = 128
            gram = jnp.where((lane[:rows] & bit) != 0, gram[bit : bit + rows], gram[:rows])
        for bit in (4, 2, 1):
            gram = jnp.where((lane[: gram.shape[0]] & bit) != 0, up_by(gram, bit), gram)
        return up_by(gram, 1)[:OFFSETS]

    @pl.loop(0, bins)
    def _(index):
        rows = pl.ds(index, every, stride=bins)
        real_x = real_own[rows, :]
        imag_x = imag_own[rows, :]
        real_y = jnp.concatenate([real_x, real_next[rows, :]], axis=1)
        imag_y = jnp.concatenate([imag_x, imag_next[rows, :]], axis=1)
        partner = jnp.concatenate([real_y, imag_y], axis=0).T[: LANES + OFFSETS].astype(BF16)
        own = jnp.concatenate(
            [
                jnp.concatenate([real_x, imag_x], axis=1),
                jnp.concatenate([imag_x, -real_x], axis=1),
            ],
            axis=0,
        ).astype(BF16)
        gram = jnp.dot(partner, own, preferred_element_type=F32)
        for part in range(2):
            value = skewed(gram[:, part * LANES : (part + 1) * LANES]) * keep
            out_ref[:, part, pl.ds(index, 1), :] = value[:, None, :]


def cross_spectra(limit, first, second, after):
    groups, windows, bins, _ = first.shape
    step = 16
    half = pl.BlockSpec((groups, windows, step, LANES), lambda b: (0, 0, b, 0))
    scratch = pltpu.VMEM((groups * windows * step, LANES), F32)
    return pl.pallas_call(
        cross_kernel,
        grid=(bins // step,),
        in_specs=[pl.BlockSpec((1, LANES), lambda b: (0, 0)), half, half, half],
        out_specs=pl.BlockSpec((OFFSETS, 2, step, LANES), lambda b: (0, 0, b, 0)),
        out_shape=jax.ShapeDtypeStruct((OFFSETS, 2, bins, LANES), F32),
        scratch_shapes=[scratch] * 4,
        compiler_params=pltpu.CompilerParams(vmem_limit_bytes=40 * 2**20),
        cost_estimate=pl.CostEstimate(
            flops=2 * bins * 192 * 96 * 256,
            bytes_accessed=6 * first.size + 4 * OFFSETS * 2 * bins * LANES,
            transcendentals=0,
        ),
        name="cross_spectra",
    )(limit, first, second, after)


def body(down, back, records, channel_live, offset_limit):
    parts = lax.axis_size("fibre")
    groups = lax.axis_size("freq")
    sums = project(down, records, parts)
    sums = lax.all_to_all(sums, "fibre", split_axis=0, concat_axis=0, tiled=True)
    first, second = whiten(channel_live[None, :], back, sums, groups)
    first = lax.all_to_all(first, "freq", split_axis=0, concat_axis=0, tiled=True)
    after = lax.ppermute(first, "fibre", [(i, i - 1) for i in range(1, parts)])
    second = lax.all_to_all(second, "freq", split_axis=0, concat_axis=0, tiled=True)
    return cross_spectra(offset_limit[None, :], first, second, after)


def solution(mesh):
    down, back = make_tables(mesh.shape["fibre"])
    down = np.concatenate(split_pair(down))
    back = split_pair(back)[0]
    return jax.shard_map(
        functools.partial(body, down, back),
        mesh=mesh,
        in_specs=(P("freq", "fibre", None), P("fibre"), P("fibre")),
        out_specs=P(None, None, "freq", "fibre"),
        check_vma=False,
    )
```

time: 444 us -> 120 us (0.27)
  waiting for transfers between devices: 149 us -> 0.01 us
  other arithmetic: 145 us -> 0 us
  local copies, waits for them, and re-layouts: 57.6 us -> 4.54 us
  Pallas kernels: 0 us -> 33.9 us
  blocking collectives: 46 us -> 77.4 us
  matrix products: 23.9 us -> 0 us
  loops' own time: 10.6 us -> 0 us
  starting transfers between devices: 10.7 us -> 3.75 us
    all_to_all x1 -> x0, waiting for transfers between devices: 133 us -> none  [body(): lax.all_to_all(records, 'fibre', split_axis=2, concat_axis=1, tiled=True)]
    reduce_sum x8 -> x0, other arithmetic: 68.9 us -> none  [one_group(): real_sum = jnp.sum(first_re * second_re + first_im * second_im, axis=0)]
    another operation x10 -> x0, other arithmetic: 67.5 us -> none
    pallas_call x0 -> x3, Pallas kernels: none -> 33.9 us  [the longest x1 23 us: cross_spectra(): pl.pallas_call(cross_kernel, grid=(bins // step,), in_specs=[pl.BlockSpec...]
    all_to_all x1 -> x3, blocking collectives: 46 us -> 77.4 us  [the longest x1 36.5 us: body(): lax.all_to_all(sums, 'fibre', split_axis=0, concat_axis=0, tiled=True)]
    all_to_all x3 -> x0, local copies, waits for them, and re-layouts: 28.1 us -> none  [the longest x2 27.6 us: body(): lax.all_to_all(records, 'fibre', split_axis=2, concat_axis=1, tiled=True)]
    dot_general x2 -> x0, matrix products: 23.9 us -> none  [the longest x1 19.2 us: body(): jnp.einsum('sj,wsc->wjc', table, channel_block, preferred_element_type=jn...]
    ppermute x1, waiting for transfers between devices: 15.8 us -> 0.01 us  [body(): after = lax.ppermute(first, 'fibre', [(i, i - 1) for i in range(1, parts)])]
  transfers between devices with their start and end apart: 2 -> 1, of which waited for: 2 -> 0; matrix products, arithmetic and copies ran while one was open for 16% -> 0% of each run, Pallas kernels for 0% -> 0%
where the time goes in v1:
time: 120 us
  blocking collectives  77.4 us (65%)
  Pallas kernels  33.9 us (28%)
  local copies, waits for them, and re-layouts  4.54 us (4%)
  starting transfers between devices  3.75 us (3%)
    all_to_all x1, blocking collectives, body(): lax.all_to_all(sums, 'fibre', split_axis=0, concat_axis=0, tiled=True)  36.5 us
    pallas_call x1, Pallas kernels, cross_spectra(): pl.pallas_call(cross_kernel, grid=(bins // step,), in_specs=[pl.BlockSpec...  23 us
    all_to_all x1, blocking collectives, body(): lax.all_to_all(first, 'freq', split_axis=0, concat_axis=0, tiled=True)  20.7 us
    all_to_all x1, blocking collectives, body(): lax.all_to_all(second, 'freq', split_axis=0, concat_axis=0, tiled=True)  20.3 us
    pallas_call x1, Pallas kernels, whiten(): pl.pallas_call(whiten_kernel, grid=(windows // 2,), in_specs=[pl.BlockSpe...  7.3 us
    unnamed x8, local copies, waits for them, and re-layouts  4.54 us
    ppermute x1, starting transfers between devices, body(): after = lax.ppermute(first, 'fibre', [(i, i - 1) for i in range(1, parts)])  3.75 us
    pallas_call x1, Pallas kernels, project(): pl.pallas_call(project_kernel, grid=(windows,), in_specs=[pl.BlockSpec((2...  3.58 us
  transfers between devices with their start and end apart: 1, of which 0 were waited for; matrix products, arithmetic and copies ran while one was open for 0% of the time, Pallas kernels for 0%

profile of v1, /device:TPU:1, one launch (start us, length us, event | category | flops | bytes accessed | tf_op | source)
XLA Modules:
  0.0 119.7 jit_solution(18176738260045300375)
XLA Ops:
  0.0 0.0 copy-start
  0.0 3.6 %copy-done = bf16[6,375,2048]{2,1,0:T(8,128)(2,1)S(1)} copy-done((bf16[6,375,2048]{2,1,0:T(8,128)(2,1)S(1)}, bf16[6,375,2048]{2,1,0:T(8,128)(2,1)}, u32[]{:S(2)}) %copy-start) | copy-done | bytes 9216024
  3.6 0.0 copy-start.1
  3.6 0.9 copy-done.1
  4.5 3.6 %project.1 = bf16[16,6,96,128]{3,2,1,0:T(8,128)(2,1)S(1)} custom-call(bf16[192,375]{1,0:T(8,128)(2,1)S(1)} %copy-done.1, bf16[6,375,2048]{2,1,0:T(8,128)(2,1)S(1)} %copy-done), custom_call_target="tpu_custom_call" | custom-call | flops 1769472000 | bytes 11575296 | tf_op jit(solution)/shard_map/project/pallas_call | solution.py:63
  8.1 0.0 copy-start.3
  8.1 36.5 %all_to_all.15.sums_ref = bf16[16,6,96,128]{3,2,1,0:T(8,128)(2,1)S(1)} all-to-all(bf16[16,6,96,128]{3,2,1,0:T(8,128)(2,1)S(1)} %project.1), channel_id=1, replica_groups=mesh['fibre'=16,'freq'=8] {'fibre'}, dimensions={0} | all-to-all | bytes 4718592 | tf_op jit(solution)/shard_map/all_to_all | solution.py:213
  44.6 0.0 copy-done.3
  44.6 0.0 copy-start.2
  44.6 7.3 %whiten.1 = (bf16[8,6,64,128]{3,2,1,0:T(8,128)(2,1)S(1)}, bf16[8,6,64,128]{3,2,1,0:T(8,128)(2,1)S(1)}) custom-call(s32[1,128]{1,0:T(1,128)S(1)} %bitcast.3, bf16[1152,1536]{1,0:T(8,128)(2,1)} %constant.5.clone.back_ref, bf16[16,6,96,128]{3,2,1,0:T(8,128)(2,1)S(1)} %all_to_all.15.sums_ref), custom_call_target="tpu_custom_call" | custom-call | flops 2717908992 | bytes 7471104 | tf_op jit(solution)/shard_map/whiten/pallas_call | solution.py:120
  52.0 20.7 %all_to_all.16.first_ref = bf16[8,6,64,128]{3,2,1,0:T(8,128)(2,1)S(1)} all-to-all(bf16[8,6,64,128]{3,2,1,0:T(8,128)(2,1)S(1)} %get-tuple-element.7), channel_id=1, replica_groups=mesh['fibre'=16,'freq'=8] {'freq'}, dimensions={0} | all-to-all | bytes 1572864 | tf_op jit(solution)/shard_map/all_to_all | solution.py:215
  72.6 3.7 %collective-permute-start = (bf16[8,6,64,128]{3,2,1,0:T(8,128)(2,1)S(1)}, bf16[8,6,64,128]{3,2,1,0:T(8,128)(2,1)S(1)}, u32[]{:S(2)}, u32[]{:S(2)}) collective-permute-start(bf16[8,6,64,128]{3,2,1,0:T(8,128)(2,1)S(1)} %all_to_all.16.first_ref), channel_id=1, source_target_pairs={{8,0},{16,8},{24,16},{32,24},{40,32},{48,40},{56,48},{64,56},{72,6... | collective-permute-start | bytes 2359304 | tf_op jit(solution)/shard_map/ppermute | solution.py:216
  76.4 20.3 %all_to_all.17.second_ref = bf16[8,6,64,128]{3,2,1,0:T(8,128)(2,1)S(1)} all-to-all(bf16[8,6,64,128]{3,2,1,0:T(8,128)(2,1)S(1)} %get-tuple-element.8), channel_id=1, replica_groups=mesh['fibre'=16,'freq'=8] {'freq'}, dimensions={0} | all-to-all | bytes 1572864 | tf_op jit(solution)/shard_map/all_to_all | solution.py:217
  96.6 0.0 collective-permute-done.next_ref
  96.6 0.0 copy-done.2
  96.6 23.0 %cross_spectra.1 = f32[64,2,64,128]{3,2,1,0:T(8,128)} custom-call(s32[1,128]{1,0:T(1,128)S(1)} %bitcast.2, bf16[8,6,64,128]{3,2,1,0:T(8,128)(2,1)S(1)} %all_to_all.16.first_ref, bf16[8,6,64,128]{3,2,1,0:T(8,128)(2,1)S(1)} %all_to_all.17.second_ref, bf16[8,6,64,128]{3,2,1,0:T(8,128)(2,1)S(1)} %collective-permute-done.next_ref), custom_call_target="tpu_custom_call" | custom-call | flops 603979776 | bytes 6553600 | tf_op jit(solution)/shard_map/cross_spectra/pallas_call | solution.py:192
Async XLA Ops:
  0.0 3.6 %copy-start = (bf16[6,375,2048]{2,1,0:T(8,128)(2,1)S(1)}, bf16[6,375,2048]{2,1,0:T(8,128)(2,1)}, u32[]{:S(2)}) copy-start(bf16[6,375,2048]{2,1,0:T(8,128)(2,1)} %records_ref.1) | copy-start | bytes 27648004
  3.6 0.9 copy-start.1
  8.1 36.5 %copy-start.3 = (s32[128]{0:T(128)S(1)}, s32[128]{0:T(128)}, u32[]{:S(2)}) copy-start(s32[128]{0:T(128)} %param.6) | copy-start | bytes 1540
  44.6 52.0 %copy-start.2 = (s32[128]{0:T(128)S(1)}, s32[128]{0:T(128)}, u32[]{:S(2)}) copy-start(s32[128]{0:T(128)} %param.7) | copy-start | bytes 1540
  72.6 24.0 %collective-permute-start = (bf16[8,6,64,128]{3,2,1,0:T(8,128)(2,1)S(1)}, bf16[8,6,64,128]{3,2,1,0:T(8,128)(2,1)S(1)}, u32[]{:S(2)}, u32[]{:S(2)}) collective-permute-start(bf16[8,6,64,128]{3,2,1,0:T(8,128)(2,1)S(1)} %all_to_all.16.first_ref), channel_id=1, source_target_pairs={{8,0},{16,8},{24,16},{32,24},{40,32},{48,40},{56,48},{64,56},{72,6... | collective-permute-start | bytes 2359304 | tf_op jit(solution)/shard_map/ppermute | solution.py:216

commit v2 on v1

--- a/solution.py
+++ b/solution.py
@@ -69,7 +69,7 @@
         ],
         out_specs=pl.BlockSpec((parts, 1, RANK, LANES), lambda w: (0, w, 0, 0)),
         out_shape=jax.ShapeDtypeStruct((parts, windows, RANK, LANES), BF16),
-        compiler_params=pltpu.CompilerParams(vmem_limit_bytes=40 * 2**20),
+        compiler_params=pltpu.CompilerParams(vmem_limit_bytes=56 * 2**20),
         cost_estimate=pl.CostEstimate(
             flops=4 * RANK * run * channels * windows,
             bytes_accessed=2 * records.size + 2 * parts * windows * RANK * LANES,
@@ -83,7 +83,7 @@
     return pltpu.roll(values, values.shape[0] - rows, axis=0)
 
 
-def whiten_kernel(live_ref, back_ref, sums_ref, first_ref, second_ref):
+def whiten_kernel(live_ref, back_ref, sums_ref, out_ref):
     parts = sums_ref.shape[0]
     columns = jnp.concatenate(
         [sums_ref[:, i].reshape(parts * RANK, LANES) for i in range(2)], axis=1
@@ -102,21 +102,20 @@
     scale = jnp.concatenate([live, live], axis=1) / (smooth + 1e-06)
     real_part = real_part[HALF : HALF + NB] * scale
     imag_part = imag_part[HALF : HALF + NB] * scale
-    groups = first_ref.shape[0]
+    groups = out_ref.shape[0]
     left = lax.broadcasted_iota(jnp.int32, (NB, LANES), 1) < LANES // 2
     for i in range(2):
         real_one = real_part[:, i * LANES : (i + 1) * LANES]
         imag_one = imag_part[:, i * LANES : (i + 1) * LANES]
         first = jnp.where(left, real_one, pltpu.roll(imag_one, LANES // 2, axis=1))
         second = jnp.where(left, pltpu.roll(real_one, LANES // 2, axis=1), imag_one)
-        first_ref[:, i] = first.astype(BF16).reshape(groups, NB // groups, LANES)
-        second_ref[:, i] = second.astype(BF16).reshape(groups, NB // groups, LANES)
+        out_ref[:, 0, i] = first.astype(BF16).reshape(groups, NB // groups, LANES)
+        out_ref[:, 1, i] = second.astype(BF16).reshape(groups, NB // groups, LANES)
 
 
 def whiten(live, back, sums, groups):
     parts, windows = sums.shape[:2]
-    shape = (groups, windows, NB // groups, LANES)
-    half = pl.BlockSpec((groups, 2, NB // groups, LANES), lambda w: (0, w, 0, 0))
+    shape = (groups, 2, windows, NB // groups, LANES)
     return pl.pallas_call(
         whiten_kernel,
         grid=(windows // 2,),
@@ -125,9 +124,9 @@
             pl.BlockSpec(back.shape, lambda w: (0, 0)),
             pl.BlockSpec((parts, 2, RANK, LANES), lambda w: (0, w, 0, 0)),
         ],
-        out_specs=[half, half],
-        out_shape=[jax.ShapeDtypeStruct(shape, BF16)] * 2,
-        compiler_params=pltpu.CompilerParams(vmem_limit_bytes=48 * 2**20),
+        out_specs=pl.BlockSpec((groups, 2, 2, NB // groups, LANES), lambda w: (0, 0, w, 0, 0)),
+        out_shape=jax.ShapeDtypeStruct(shape, BF16),
+        compiler_params=pltpu.CompilerParams(vmem_limit_bytes=28 * 2**20),
         cost_estimate=pl.CostEstimate(
             flops=2 * back.size * windows * LANES,
             bytes_accessed=2 * (back.size + sums.size + 2 * windows * NB * LANES),
@@ -137,13 +136,13 @@
     )(live, back, sums)
 
 
-def cross_kernel(limit_ref, first_ref, second_ref, next_ref, out_ref, real_own, imag_own, real_next, imag_next):
-    groups, windows, bins, _ = first_ref.shape
+def cross_kernel(limit_ref, halves_ref, next_ref, out_ref, real_own, imag_own, real_next, imag_next):
+    groups, windows, bins, _ = next_ref.shape
     every = groups * windows
     half = LANES // 2
     left = lax.broadcasted_iota(jnp.int32, (every * bins, LANES), 1) < half
-    first = first_ref[...].astype(F32).reshape(every * bins, LANES)
-    second = second_ref[...].astype(F32).reshape(every * bins, LANES)
+    first = halves_ref[:, 0].astype(F32).reshape(every * bins, LANES)
+    second = halves_ref[:, 1].astype(F32).reshape(every * bins, LANES)
     real_own[...] = jnp.where(left, first, pltpu.roll(second, half, axis=1))
     imag_own[...] = jnp.where(left, pltpu.roll(first, half, axis=1), second)
     after = next_ref[...].astype(F32).reshape(every * bins, LANES)
@@ -159,11 +158,15 @@
             if bit == 64:
                 rows = 128
             gram = jnp.where((lane[:rows] & bit) != 0, gram[bit : bit + rows], gram[:rows])
-        for bit in (4, 2, 1):
-            gram = jnp.where((lane[: gram.shape[0]] & bit) != 0, up_by(gram, bit), gram)
-        return up_by(gram, 1)[:OFFSETS]
-
-    @pl.loop(0, bins)
+        turn = (lane[:8] & 7) + 1
+        spot = lax.broadcasted_iota(jnp.int32, (8, LANES), 0) + turn
+        pieces = []
+        for row in range(0, OFFSETS + 8, 8):
+            pieces.append(jnp.take_along_axis(gram[row : row + 8], spot & 7, axis=0))
+        merged = [jnp.where(spot < 8, pieces[p], pieces[p + 1]) for p in range(OFFSETS // 8)]
+        return jnp.concatenate(merged, axis=0)
+
+    @pl.loop(0, bins, unroll=16)
     def _(index):
         rows = pl.ds(index, every, stride=bins)
         real_x = real_own[rows, :]
@@ -181,29 +184,31 @@
         gram = jnp.dot(partner, own, preferred_element_type=F32)
         for part in range(2):
             value = skewed(gram[:, part * LANES : (part + 1) * LANES]) * keep
-            out_ref[:, part, pl.ds(index, 1), :] = value[:, None, :]
-
-
-def cross_spectra(limit, first, second, after):
-    groups, windows, bins, _ = first.shape
+            flat = out_ref.reshape(OFFSETS * 2 * bins, LANES)
+            flat[pl.ds(part * bins + index, OFFSETS, stride=2 * bins), :] = value
+
+
+def cross_spectra(limit, halves, after):
+    groups, windows, bins, _ = after.shape
     step = 16
+    own = pl.BlockSpec((groups, 2, windows, step, LANES), lambda b: (0, 0, 0, b, 0))
     half = pl.BlockSpec((groups, windows, step, LANES), lambda b: (0, 0, b, 0))
     scratch = pltpu.VMEM((groups * windows * step, LANES), F32)
     return pl.pallas_call(
         cross_kernel,
         grid=(bins // step,),
-        in_specs=[pl.BlockSpec((1, LANES), lambda b: (0, 0)), half, half, half],
+        in_specs=[pl.BlockSpec((1, LANES), lambda b: (0, 0)), own, half],
         out_specs=pl.BlockSpec((OFFSETS, 2, step, LANES), lambda b: (0, 0, b, 0)),
         out_shape=jax.ShapeDtypeStruct((OFFSETS, 2, bins, LANES), F32),
         scratch_shapes=[scratch] * 4,
-        compiler_params=pltpu.CompilerParams(vmem_limit_bytes=40 * 2**20),
+        compiler_params=pltpu.CompilerParams(vmem_limit_bytes=20 * 2**20),
         cost_estimate=pl.CostEstimate(
             flops=2 * bins * 192 * 96 * 256,
-            bytes_accessed=6 * first.size + 4 * OFFSETS * 2 * bins * LANES,
+            bytes_accessed=6 * after.size + 4 * OFFSETS * 2 * bins * LANES,
             transcendentals=0,
         ),
         name="cross_spectra",
-    )(limit, first, second, after)
+    )(limit, halves, after)
 
 
 def body(down, back, records, channel_live, offset_limit):
@@ -211,11 +216,10 @@
     groups = lax.axis_size("freq")
     sums = project(down, records, parts)
     sums = lax.all_to_all(sums, "fibre", split_axis=0, concat_axis=0, tiled=True)
-    first, second = whiten(channel_live[None, :], back, sums, groups)
-    first = lax.all_to_all(first, "freq", split_axis=0, concat_axis=0, tiled=True)
-    after = lax.ppermute(first, "fibre", [(i, i - 1) for i in range(1, parts)])
-    second = lax.all_to_all(second, "freq", split_axis=0, concat_axis=0, tiled=True)
-    return cross_spectra(offset_limit[None, :], first, second, after)
+    halves = whiten(channel_live[None, :], back, sums, groups)
+    halves = lax.all_to_all(halves, "freq", split_axis=0, concat_axis=0, tiled=True)
+    after = lax.ppermute(halves[:, 0], "fibre", [(i, i - 1) for i in range(1, parts)])
+    return cross_spectra(offset_limit[None, :], halves, after)
 
 
 def solution(mesh):

time: 120 us -> 101 us (0.84)
  Pallas kernels: 33.9 us -> 21.2 us
  blocking collectives: 77.4 us -> 66.1 us
  waiting for transfers between devices: 0.01 us -> 9.57 us
  local copies, waits for them, and re-layouts: 4.54 us -> 0.07 us
    pallas_call x1, Pallas kernels: 23 us -> 8.03 us  [cross_spectra(): pl.pallas_call(cross_kernel, grid=(bins // step,), in_specs=[pl.BlockSpec...]
    all_to_all x2 -> x1, blocking collectives: 40.9 us -> 29.1 us  [body(): lax.all_to_all(halves, 'freq', split_axis=0, concat_axis=0, tiled=True)]
    ppermute x1, waiting for transfers between devices: 0.01 us -> 9.57 us  [body(): lax.ppermute(halves[:, 0], 'fibre', [(i, i - 1) for i in range(1, parts)])]
    unnamed x8 -> x6, local copies, waits for them, and re-layouts: 4.54 us -> 0.01 us
    pallas_call x1, Pallas kernels: 3.58 us -> 7.8 us  [project(): pl.pallas_call(project_kernel, grid=(windows,), in_specs=[pl.BlockSpec((2...]
    pallas_call x1, Pallas kernels: 7.3 us -> 5.39 us  [whiten(): pl.pallas_call(whiten_kernel, grid=(windows // 2,), in_specs=[pl.BlockSpe...]
  transfers between devices with their start and end apart: 1 -> 1, of which waited for: 0 -> 1; matrix products, arithmetic and copies ran while one was open for 0% -> 0% of each run, Pallas kernels for 0% -> 0%
where the time goes in v2:
time: 101 us
  blocking collectives  66.1 us (65%)
  Pallas kernels  21.2 us (21%)
  waiting for transfers between devices  9.57 us (9%)
  starting transfers between devices  3.76 us (4%)
    all_to_all x1, blocking collectives, body(): lax.all_to_all(sums, 'fibre', split_axis=0, concat_axis=0, tiled=True)  37 us
    all_to_all x1, blocking collectives, body(): lax.all_to_all(halves, 'freq', split_axis=0, concat_axis=0, tiled=True)  29.1 us
    ppermute x1, waiting for transfers between devices, body(): lax.ppermute(halves[:, 0], 'fibre', [(i, i - 1) for i in range(1, parts)])  9.57 us
    pallas_call x1, Pallas kernels, cross_spectra(): pl.pallas_call(cross_kernel, grid=(bins // step,), in_specs=[pl.BlockSpec...  8.03 us
    pallas_call x1, Pallas kernels, project(): pl.pallas_call(project_kernel, grid=(windows,), in_specs=[pl.BlockSpec((2...  7.8 us
    pallas_call x1, Pallas kernels, whiten(): pl.pallas_call(whiten_kernel, grid=(windows // 2,), in_specs=[pl.BlockSpe...  5.39 us
    ppermute x1, starting transfers between devices, body(): lax.ppermute(halves[:, 0], 'fibre', [(i, i - 1) for i in range(1, parts)])  3.76 us
  transfers between devices with their start and end apart: 1, of which 1 were waited for; matrix products, arithmetic and copies ran while one was open for 0% of the time, Pallas kernels for 0%

profile of v2, /device:TPU:1, one launch (start us, length us, event | category | flops | bytes accessed | tf_op | source)
XLA Modules:
  0.0 100.7 jit_solution(14018592018524960966)
XLA Ops:
  0.0 7.8 %project.1 = bf16[16,6,96,128]{3,2,1,0:T(8,128)(2,1)} custom-call(bf16[192,375]{1,0:T(8,128)(2,1)} %constant.4.clone.down_ref, bf16[6,375,2048]{2,1,0:T(8,128)(2,1)} %records_ref.1), custom_call_target="tpu_custom_call" | custom-call | flops 1769472000 | bytes 11575296 | tf_op jit(solution)/shard_map/project/pallas_call | solution.py:63
  7.8 0.0 copy-start.1
  7.8 0.0 copy-start.2
  7.8 37.0 %all_to_all.10.sums_ref = bf16[16,6,96,128]{3,2,1,0:T(8,128)(2,1)S(1)} all-to-all(bf16[16,6,96,128]{3,2,1,0:T(8,128)(2,1)} %project.1), channel_id=1, replica_groups=mesh['fibre'=16,'freq'=8] {'fibre'}, dimensions={0} | all-to-all | bytes 4718592 | tf_op jit(solution)/shard_map/all_to_all | solution.py:218
  44.8 0.0 copy-done.1
  44.8 0.0 copy-done.2
  44.8 5.4 %whiten.1 = bf16[8,2,6,64,128]{4,3,2,1,0:T(8,128)(2,1)S(1)} custom-call(s32[1,128]{1,0:T(1,128)S(1)} %bitcast.7, bf16[1152,1536]{1,0:T(8,128)(2,1)S(1)} %copy-done.2, bf16[16,6,96,128]{3,2,1,0:T(8,128)(2,1)S(1)} %all_to_all.10.sums_ref), custom_call_target="tpu_custom_call" | custom-call | flops 2717908992 | bytes 7471104 | tf_op jit(solution)/shard_map/whiten/pallas_call | solution.py:119
  50.2 0.0 copy-start
  50.2 29.1 %all_to_all.11.halves_ref = bf16[8,2,6,64,128]{4,3,2,1,0:T(8,128)(2,1)S(1)} all-to-all(bf16[8,2,6,64,128]{4,3,2,1,0:T(8,128)(2,1)S(1)} %whiten.1), channel_id=1, replica_groups=mesh['fibre'=16,'freq'=8] {'freq'}, dimensions={0} | all-to-all | bytes 3145728 | tf_op jit(solution)/shard_map/all_to_all | solution.py:220
  79.3 0.1 slice_bitcast_fusion
  79.3 3.8 %collective-permute-start = (bf16[8,6,64,128]{3,2,1,0:T(8,128)(2,1)S(1)}, bf16[8,6,64,128]{3,2,1,0:T(8,128)(2,1)S(1)}, u32[]{:S(2)}, u32[]{:S(2)}) collective-permute-start(bf16[8,6,64,128]{3,2,1,0:T(8,128)(2,1)S(1)} %slice_bitcast_fusion), channel_id=1, source_target_pairs={{8,0},{16,8},{24,16},{32,24},{40,32},{48,40},{56,48},{64,56},{72,6... | collective-permute-start | bytes 2359304 | tf_op jit(solution)/shard_map/ppermute | solution.py:221
  83.1 9.6 %collective-permute-done.next_ref = bf16[8,6,64,128]{3,2,1,0:T(8,128)(2,1)S(1)} collective-permute-done((bf16[8,6,64,128]{3,2,1,0:T(8,128)(2,1)S(1)}, bf16[8,6,64,128]{3,2,1,0:T(8,128)(2,1)S(1)}, u32[]{:S(2)}, u32[]{:S(2)}) %collective-permute-start) | collective-permute-done | bytes 786464 | tf_op jit(solution)/shard_map/ppermute | solution.py:221
  92.7 0.0 copy-done
  92.7 8.0 %cross_spectra.1 = f32[64,2,64,128]{3,2,1,0:T(8,128)} custom-call(s32[1,128]{1,0:T(1,128)S(1)} %bitcast.6, bf16[8,2,6,64,128]{4,3,2,1,0:T(8,128)(2,1)S(1)} %all_to_all.11.halves_ref, bf16[8,6,64,128]{3,2,1,0:T(8,128)(2,1)S(1)} %collective-permute-done.next_ref), custom_call_target="tpu_custom_call" | custom-call | flops 603979776 | bytes 6553600 | tf_op jit(solution)/shard_map/cross_spectra/pallas_call | solution.py:197
Async XLA Ops:
  7.8 37.0 %copy-start.1 = (s32[128]{0:T(128)S(1)}, s32[128]{0:T(128)}, u32[]{:S(2)}) copy-start(s32[128]{0:T(128)} %param.6) | copy-start | bytes 1540
  7.8 37.0 %copy-start.2 = (bf16[1152,1536]{1,0:T(8,128)(2,1)S(1)}, bf16[1152,1536]{1,0:T(8,128)(2,1)}, u32[]{:S(2)}) copy-start(bf16[1152,1536]{1,0:T(8,128)(2,1)} %constant.5.clone.back_ref) | copy-start | bytes 10616836
  50.2 42.5 %copy-start = (s32[128]{0:T(128)S(1)}, s32[128]{0:T(128)}, u32[]{:S(2)}) copy-start(s32[128]{0:T(128)} %param.7) | copy-start | bytes 1540
  79.3 13.3 %collective-permute-start = (bf16[8,6,64,128]{3,2,1,0:T(8,128)(2,1)S(1)}, bf16[8,6,64,128]{3,2,1,0:T(8,128)(2,1)S(1)}, u32[]{:S(2)}, u32[]{:S(2)}) collective-permute-start(bf16[8,6,64,128]{3,2,1,0:T(8,128)(2,1)S(1)} %slice_bitcast_fusion), channel_id=1, source_target_pairs={{8,0},{16,8},{24,16},{32,24},{40,32},{48,40},{56,48},{64,56},{72,6... | collective-permute-start | bytes 2359304 | tf_op jit(solution)/shard_map/ppermute | solution.py:221

commit v3 on v2

--- a/solution.py
+++ b/solution.py
@@ -15,6 +15,7 @@
 OFFSETS = 64
 BINS = NB + 2 * HALF
 RANK = 96
+PITCH = 24
 LANES = 128
 F32 = jnp.float32
 BF16 = jnp.bfloat16
@@ -47,28 +48,39 @@
     return down, back.reshape(2 * BINS, parts * RANK)
 
 
-def project_kernel(down_ref, records_ref, out_ref):
-    parts = out_ref.shape[0]
+def project_kernel(down_ref, records_ref, out_ref, held, arrived):
+    parts, windows = out_ref.shape[:2]
     wide = 4
-    for start in range(0, parts, wide):
-        block = records_ref[0, :, start * LANES : (start + wide) * LANES]
-        both = jnp.dot(down_ref[...], block, preferred_element_type=F32)
-        sums = (both[:RANK] + both[RANK:]).astype(BF16)
-        for part in range(wide):
-            out_ref[start + part, 0] = sums[:, part * LANES : (part + 1) * LANES]
+
+    def fetch(window):
+        return pltpu.make_async_copy(records_ref.at[window], held.at[window], arrived.at[window])
+
+    for window in range(windows):
+        fetch(window).start()
+    for window in range(windows):
+        fetch(window).wait()
+        for start in range(0, parts, wide):
+            block = held[window, :, start * LANES : (start + wide) * LANES]
+            both = jnp.dot(down_ref[...], block, preferred_element_type=F32)
+            sums = (both[:RANK] + both[RANK:]).astype(BF16)
+            for part in range(wide):
+                out_ref[start + part, window] = sums[:, part * LANES : (part + 1) * LANES]
 
 
 def project(down, records, parts):
     windows, run, channels = records.shape
     return pl.pallas_call(
         project_kernel,
-        grid=(windows,),
         in_specs=[
-            pl.BlockSpec((2 * RANK, run), lambda w: (0, 0)),
-            pl.BlockSpec((1, run, channels), lambda w: (w, 0, 0)),
-        ],
-        out_specs=pl.BlockSpec((parts, 1, RANK, LANES), lambda w: (0, w, 0, 0)),
+            pl.BlockSpec(memory_space=pltpu.VMEM),
+            pl.BlockSpec(memory_space=pltpu.HBM),
+        ],
+        out_specs=pl.BlockSpec(memory_space=pltpu.VMEM),
         out_shape=jax.ShapeDtypeStruct((parts, windows, RANK, LANES), BF16),
+        scratch_shapes=[
+            pltpu.VMEM(records.shape, BF16),
+            pltpu.SemaphoreType.DMA((windows,)),
+        ],
         compiler_params=pltpu.CompilerParams(vmem_limit_bytes=56 * 2**20),
         cost_estimate=pl.CostEstimate(
             flops=4 * RANK * run * channels * windows,
@@ -136,44 +148,51 @@
     )(live, back, sums)
 
 
-def cross_kernel(limit_ref, halves_ref, next_ref, out_ref, real_own, imag_own, real_next, imag_next):
-    groups, windows, bins, _ = next_ref.shape
+def swapped(tiles):
+    row = lax.broadcasted_iota(jnp.int32, (8, LANES), 0)
+    moved = [tiles[0]] + [pltpu.roll(tiles[j], j, axis=0) for j in range(1, 8)]
+    for bit in (1, 2, 4):
+        take = (row & bit) != 0
+        moved = [jnp.where(take, moved[(j + bit) % 8], moved[j]) for j in range(8)]
+    return [moved[0]] + [pltpu.roll(moved[8 - i], 8 - i, axis=0) for i in range(1, 8)]
+
+
+def own_kernel(limit_ref, halves_ref, part_ref, later_ref, first_all, second_all):
+    groups, _, windows, bins, _ = halves_ref.shape
     every = groups * windows
     half = LANES // 2
-    left = lax.broadcasted_iota(jnp.int32, (every * bins, LANES), 1) < half
-    first = halves_ref[:, 0].astype(F32).reshape(every * bins, LANES)
-    second = halves_ref[:, 1].astype(F32).reshape(every * bins, LANES)
-    real_own[...] = jnp.where(left, first, pltpu.roll(second, half, axis=1))
-    imag_own[...] = jnp.where(left, pltpu.roll(first, half, axis=1), second)
-    after = next_ref[...].astype(F32).reshape(every * bins, LANES)
-    real_next[...] = after
-    imag_next[...] = pltpu.roll(after, half, axis=1)
+    first_all[:, :bins] = halves_ref[:, 0].astype(F32).reshape(every, bins, LANES)
+    second_all[:, :bins] = halves_ref[:, 1].astype(F32).reshape(every, bins, LANES)
+    first_rows = first_all.reshape(every * PITCH, LANES)
+    second_rows = second_all.reshape(every * PITCH, LANES)
+    left = lax.broadcasted_iota(jnp.int32, (every, LANES), 1) < half
     offsets = lax.broadcasted_iota(jnp.int32, (OFFSETS, LANES), 0) + 1
     keep = (offsets <= limit_ref[...]).astype(F32)
     lane = lax.broadcasted_iota(jnp.int32, (LANES, LANES), 1)
+    turn = (lane[:8] & 7) + 1
+    spot = lax.broadcasted_iota(jnp.int32, (8, LANES), 0) + turn
 
     def skewed(gram):
+        gram = jnp.concatenate([gram, jnp.zeros((OFFSETS, LANES), F32)], axis=0)
         for bit in (64, 32, 16, 8):
-            rows = gram.shape[0] - bit
-            if bit == 64:
-                rows = 128
+            rows = min(gram.shape[0] - bit, LANES)
             gram = jnp.where((lane[:rows] & bit) != 0, gram[bit : bit + rows], gram[:rows])
-        turn = (lane[:8] & 7) + 1
-        spot = lax.broadcasted_iota(jnp.int32, (8, LANES), 0) + turn
-        pieces = []
-        for row in range(0, OFFSETS + 8, 8):
-            pieces.append(jnp.take_along_axis(gram[row : row + 8], spot & 7, axis=0))
+        pieces = [
+            jnp.take_along_axis(gram[row : row + 8], spot & 7, axis=0)
+            for row in range(0, OFFSETS + 8, 8)
+        ]
         merged = [jnp.where(spot < 8, pieces[p], pieces[p + 1]) for p in range(OFFSETS // 8)]
         return jnp.concatenate(merged, axis=0)
 
     @pl.loop(0, bins, unroll=16)
     def _(index):
-        rows = pl.ds(index, every, stride=bins)
-        real_x = real_own[rows, :]
-        imag_x = imag_own[rows, :]
-        real_y = jnp.concatenate([real_x, real_next[rows, :]], axis=1)
-        imag_y = jnp.concatenate([imag_x, imag_next[rows, :]], axis=1)
-        partner = jnp.concatenate([real_y, imag_y], axis=0).T[: LANES + OFFSETS].astype(BF16)
+        rows = pl.ds(index, every, stride=PITCH)
+        first = first_rows[rows, :]
+        second = second_rows[rows, :]
+        turned = pltpu.roll(second, half, axis=1)
+        real_x = jnp.where(left, first, turned)
+        imag_x = jnp.where(left, pltpu.roll(first, half, axis=1), second)
+        partner = jnp.concatenate([real_x, imag_x], axis=0).T.astype(BF16)
         own = jnp.concatenate(
             [
                 jnp.concatenate([real_x, imag_x], axis=1),
@@ -184,42 +203,144 @@
         gram = jnp.dot(partner, own, preferred_element_type=F32)
         for part in range(2):
             value = skewed(gram[:, part * LANES : (part + 1) * LANES]) * keep
-            flat = out_ref.reshape(OFFSETS * 2 * bins, LANES)
-            flat[pl.ds(part * bins + index, OFFSETS, stride=2 * bins), :] = value
-
-
-def cross_spectra(limit, halves, after):
+            part_ref[pl.ds(index, 1), part] = value[None]
+        late = jnp.concatenate([second, jnp.where(left, turned, -turned)], axis=0)
+        later_ref[pl.ds(index, 1)] = late.astype(BF16)[None]
+
+
+def next_kernel(limit_ref, part_ref, later_ref, next_ref, out_ref, next_all, held, sent):
+    groups, windows, _, _ = next_ref.shape
+    steps, bins = held.shape[0], held.shape[3]
+    every = groups * windows
+    half = LANES // 2
+    lane = lax.broadcasted_iota(jnp.int32, (half, LANES), 1)
+    back = half - 1 - (lane & (half - 1))
+    row = lax.broadcasted_iota(jnp.int32, (8, LANES), 0)
+    spot = row - (back[:8] & 7)
+
+    def lowered(gram):
+        for bit in (32, 16, 8):
+            moved = jnp.concatenate([jnp.zeros((bit, LANES), F32), gram[: half - bit]], axis=0)
+            gram = jnp.where((back & bit) != 0, moved, gram)
+        pieces = [jnp.zeros((8, LANES), F32)] + [
+            jnp.take_along_axis(gram[at : at + 8], spot & 7, axis=0) for at in range(0, half, 8)
+        ]
+        merged = [jnp.where(spot >= 0, pieces[p + 1], pieces[p]) for p in range(half // 8)]
+        return jnp.concatenate(merged, axis=0)
+
+    offsets = lax.broadcasted_iota(jnp.int32, (OFFSETS, LANES), 0) + 1
+    lanes = lax.broadcasted_iota(jnp.int32, (OFFSETS, LANES), 1)
+    keep = ((offsets <= limit_ref[...]) & (lanes >= half)).astype(F32)
+
+    def send(step):
+        where = pl.ds(pl.multiple_of(step * bins, bins), bins)
+        return pltpu.make_async_copy(held.at[step], out_ref.at[:, :, where], sent.at[step])
+
+    @pl.loop(0, steps)
+    def _(step):
+        base = pl.multiple_of(step * bins, bins)
+        after_all = next_ref[:, :, pl.ds(base, bins)]
+        next_all[:, :bins] = after_all.astype(F32).reshape(every, bins, LANES)
+        next_rows = next_all.reshape(every * PITCH, LANES)
+
+        def next_part(index):
+            after = next_rows[pl.ds(index, every, stride=PITCH), :]
+            partner = jnp.concatenate([after, pltpu.roll(after, half, axis=1)], axis=0)
+            partner = partner.T[:half].astype(BF16)
+            return lowered(jnp.dot(partner, later_ref[base + index], preferred_element_type=F32))
+
+        for start in range(0, bins, 8):
+            extra = [next_part(start + at) for at in range(8)]
+            for part in range(2):
+                for tile in range(0, OFFSETS, 8):
+                    sums = []
+                    for at in range(8):
+                        value = extra[at][tile : tile + 8]
+                        if part == 0:
+                            value = pltpu.roll(value, half, axis=1)
+                        value = value * keep[tile : tile + 8]
+                        own = part_ref[base + start + at, part, tile : tile + 8]
+                        sums.append(own + value)
+                    for at, value in enumerate(swapped(sums)):
+                        held[step, tile + at, part, start : start + 8] = value
+        send(step).start()
+
+    for step in range(steps):
+        send(step).wait()
+
+
+def own_spectra(limit, halves):
+    groups, _, windows, bins, _ = halves.shape
+    step = 16
+    every = groups * windows
+    scratch = pltpu.VMEM((every, PITCH, LANES), F32)
+    return pl.pallas_call(
+        own_kernel,
+        grid=(bins // step,),
+        in_specs=[
+            pl.BlockSpec((1, LANES), lambda b: (0, 0)),
+            pl.BlockSpec((groups, 2, windows, step, LANES), lambda b: (0, 0, 0, b, 0)),
+        ],
+        out_specs=[
+            pl.BlockSpec((step, 2, OFFSETS, LANES), lambda b: (b, 0, 0, 0)),
+            pl.BlockSpec((step, 2 * every, LANES), lambda b: (b, 0, 0)),
+        ],
+        out_shape=[
+            jax.ShapeDtypeStruct((bins, 2, OFFSETS, LANES), F32),
+            jax.ShapeDtypeStruct((bins, 2 * every, LANES), BF16),
+        ],
+        scratch_shapes=[scratch] * 2,
+        compiler_params=pltpu.CompilerParams(vmem_limit_bytes=20 * 2**20),
+        cost_estimate=pl.CostEstimate(
+            flops=2 * bins * 128 * 96 * 256,
+            bytes_accessed=4 * halves.size + 4 * OFFSETS * 2 * bins * LANES,
+            transcendentals=0,
+        ),
+        name="own_spectra",
+    )(limit, halves)
+
+
+def next_spectra(limit, own, later, after):
     groups, windows, bins, _ = after.shape
     step = 16
-    own = pl.BlockSpec((groups, 2, windows, step, LANES), lambda b: (0, 0, 0, b, 0))
-    half = pl.BlockSpec((groups, windows, step, LANES), lambda b: (0, 0, b, 0))
-    scratch = pltpu.VMEM((groups * windows * step, LANES), F32)
+    every = groups * windows
+    resident = pl.BlockSpec(memory_space=pltpu.VMEM)
     return pl.pallas_call(
-        cross_kernel,
-        grid=(bins // step,),
-        in_specs=[pl.BlockSpec((1, LANES), lambda b: (0, 0)), own, half],
-        out_specs=pl.BlockSpec((OFFSETS, 2, step, LANES), lambda b: (0, 0, b, 0)),
+        next_kernel,
+        in_specs=[resident] * 4,
+        out_specs=pl.BlockSpec(memory_space=pl.ANY),
         out_shape=jax.ShapeDtypeStruct((OFFSETS, 2, bins, LANES), F32),
-        scratch_shapes=[scratch] * 4,
+        scratch_shapes=[
+            pltpu.VMEM((every, PITCH, LANES), F32),
+            pltpu.VMEM((bins // step, OFFSETS, 2, step, LANES), F32),
+            pltpu.SemaphoreType.DMA((bins // step,)),
+        ],
         compiler_params=pltpu.CompilerParams(vmem_limit_bytes=20 * 2**20),
         cost_estimate=pl.CostEstimate(
-            flops=2 * bins * 192 * 96 * 256,
-            bytes_accessed=6 * after.size + 4 * OFFSETS * 2 * bins * LANES,
+            flops=2 * bins * 64 * 96 * 128,
+            bytes_accessed=2 * after.size + 8 * OFFSETS * 2 * bins * LANES,
             transcendentals=0,
         ),
-        name="cross_spectra",
-    )(limit, halves, after)
+        name="next_spectra",
+    )(limit, own, later, after)
+
+
+def exchanged(blocks, axis):
+    flat = blocks.reshape(blocks.shape[0], -1, LANES)
+    flat = lax.all_to_all(flat, axis, split_axis=0, concat_axis=0, tiled=True)
+    return flat.reshape(blocks.shape)
 
 
 def body(down, back, records, channel_live, offset_limit):
     parts = lax.axis_size("fibre")
     groups = lax.axis_size("freq")
     sums = project(down, records, parts)
-    sums = lax.all_to_all(sums, "fibre", split_axis=0, concat_axis=0, tiled=True)
+    sums = exchanged(sums, "fibre")
     halves = whiten(channel_live[None, :], back, sums, groups)
-    halves = lax.all_to_all(halves, "freq", split_axis=0, concat_axis=0, tiled=True)
+    halves = exchanged(halves, "freq")
     after = lax.ppermute(halves[:, 0], "fibre", [(i, i - 1) for i in range(1, parts)])
-    return cross_spectra(offset_limit[None, :], halves, after)
+    own, later = own_spectra(offset_limit[None, :], halves)
+    return next_spectra(offset_limit[None, :], own, later, after)
 
 
 def solution(mesh):

time: 101 us -> 97 us (0.960)
  waiting for transfers between devices: 9.57 us -> 5.63 us
    ppermute x1, waiting for transfers between devices: 9.57 us -> 5.63 us  [body(): lax.ppermute(halves[:, 0], 'fibre', [(i, i - 1) for i in range(1, parts)])]
    pallas_call x2 -> x3, Pallas kernels: 15.8 us -> 15.8 us  [the longest x1 7.2 us: project(): pl.pallas_call(project_kernel, in_specs=[pl.BlockSpec(memory_space=pltpu....]
  transfers between devices with their start and end apart: 1 -> 1, of which waited for: 1 -> 1; matrix products, arithmetic and copies ran while one was open for 0% -> 0% of each run, Pallas kernels for 0% -> 4%
where the time goes in v3:
time: 97 us; the launch traced here: 96.8 us
  blocking collectives  66.1 us (68%)
  Pallas kernels  21.2 us (22%)
  waiting for transfers between devices  5.63 us (6%)
  starting transfers between devices  3.76 us (4%)
    all_to_all x2, blocking collectives, exchanged(): flat = lax.all_to_all(flat, axis, split_axis=0, concat_axis=0, tiled=True)  66.1 us
    pallas_call x1, Pallas kernels, project(): pl.pallas_call(project_kernel, in_specs=[pl.BlockSpec(memory_space=pltpu....  7.2 us
    ppermute x1, waiting for transfers between devices, body(): lax.ppermute(halves[:, 0], 'fibre', [(i, i - 1) for i in range(1, parts)])  5.63 us
    pallas_call x1, Pallas kernels, whiten(): pl.pallas_call(whiten_kernel, grid=(windows // 2,), in_specs=[pl.BlockSpe...  5.4 us
    pallas_call x1, Pallas kernels, next_spectra(): pl.pallas_call(next_kernel, in_specs=[resident] * 4, out_specs=pl.BlockSp...  4.64 us
    pallas_call x1, Pallas kernels, own_spectra(): pl.pallas_call(own_kernel, grid=(bins // step,), in_specs=[pl.BlockSpec((...  3.93 us
    ppermute x1, starting transfers between devices, body(): lax.ppermute(halves[:, 0], 'fibre', [(i, i - 1) for i in range(1, parts)])  3.76 us
  transfers between devices with their start and end apart: 1, of which 1 were waited for; matrix products, arithmetic and copies ran while one was open for 0% of the time, Pallas kernels for 4%

profile of v3, /device:TPU:1, one launch (start us, length us, event | category | flops | bytes accessed | tf_op | source)
XLA Modules:
  0.0 96.8 jit_solution(14127650331882950446)
XLA Ops:
  0.0 7.2 %project.1 = bf16[16,6,96,128]{3,2,1,0:T(8,128)(2,1)} custom-call(bf16[192,375]{1,0:T(8,128)(2,1)} %constant.4.clone.down_ref, bf16[6,375,2048]{2,1,0:T(8,128)(2,1)} %records_ref.1), custom_call_target="tpu_custom_call" | custom-call | flops 1769472000 | bytes 11575296 | tf_op jit(solution)/shard_map/project/pallas_call | solution.py:72
  7.2 0.0 copy-start.1
  7.2 0.0 copy-start.2
  7.2 37.0 %all_to_all.10 = bf16[16,576,128]{2,1,0:T(8,128)(2,1)S(1)} all-to-all(bf16[16,576,128]{2,1,0:T(8,128)(2,1)} %bitcast.17), channel_id=1, replica_groups=mesh['fibre'=16,'freq'=8] {'fibre'}, dimensions={0} | all-to-all | bytes 4718592 | tf_op jit(solution)/shard_map/all_to_all | solution.py:330
  44.2 0.0 copy-done.1
  44.2 0.0 copy-done.2
  44.2 5.4 %whiten.1 = bf16[8,2,6,64,128]{4,3,2,1,0:T(8,128)(2,1)S(1)} custom-call(s32[1,128]{1,0:T(1,128)S(1)} %bitcast.16, bf16[1152,1536]{1,0:T(8,128)(2,1)S(1)} %copy-done.2, bf16[16,6,96,128]{3,2,1,0:T(8,128)(2,1)S(1)} %bitcast.12), custom_call_target="tpu_custom_call" | custom-call | flops 2717908992 | bytes 7471104 | tf_op jit(solution)/shard_map/whiten/pallas_call | solution.py:131
  49.6 0.0 copy-start
  49.6 29.1 %all_to_all.11 = bf16[8,768,128]{2,1,0:T(8,128)(2,1)S(1)} all-to-all(bf16[8,768,128]{2,1,0:T(8,128)(2,1)S(1)} %bitcast.13), channel_id=1, replica_groups=mesh['fibre'=16,'freq'=8] {'freq'}, dimensions={0} | all-to-all | bytes 3145728 | tf_op jit(solution)/shard_map/all_to_all | solution.py:330
  78.7 0.1 slice_bitcast_fusion
  78.8 3.8 %collective-permute-start = (bf16[8,6,64,128]{3,2,1,0:T(8,128)(2,1)S(1)}, bf16[8,6,64,128]{3,2,1,0:T(8,128)(2,1)S(1)}, u32[]{:S(2)}, u32[]{:S(2)}) collective-permute-start(bf16[8,6,64,128]{3,2,1,0:T(8,128)(2,1)S(1)} %slice_bitcast_fusion), channel_id=1, source_target_pairs={{8,0},{16,8},{24,16},{32,24},{40,32},{48,40},{56,48},{64,56},{72,6... | collective-permute-start | bytes 2359304 | tf_op jit(solution)/shard_map/ppermute | solution.py:341
  82.5 0.0 copy-done
  82.6 3.9 %own_spectra.1 = (f32[64,2,64,128]{3,2,1,0:T(8,128)S(1)}, bf16[64,96,128]{2,1,0:T(8,128)(2,1)S(1)}) custom-call(s32[1,128]{1,0:T(1,128)S(1)} %bitcast.14, bf16[8,2,6,64,128]{4,3,2,1,0:T(8,128)(2,1)S(1)} %bitcast.11), custom_call_target="tpu_custom_call" | custom-call | flops 402653184 | bytes 7340032 | tf_op jit(solution)/shard_map/own_spectra/pallas_call | solution.py:277
  86.5 5.6 %collective-permute-done.next_ref = bf16[8,6,64,128]{3,2,1,0:T(8,128)(2,1)S(1)} collective-permute-done((bf16[8,6,64,128]{3,2,1,0:T(8,128)(2,1)S(1)}, bf16[8,6,64,128]{3,2,1,0:T(8,128)(2,1)S(1)}, u32[]{:S(2)}, u32[]{:S(2)}) %collective-permute-start) | collective-permute-done | bytes 786464 | tf_op jit(solution)/shard_map/ppermute | solution.py:341
  92.1 4.6 %next_spectra.1 = f32[64,2,64,128]{3,2,1,0:T(8,128)} custom-call(s32[1,128]{1,0:T(1,128)S(1)} %bitcast.15, f32[64,2,64,128]{3,2,1,0:T(8,128)S(1)} %get-tuple-element.7.part_ref, bf16[64,96,128]{2,1,0:T(8,128)(2,1)S(1)} %get-tuple-element.8.later_ref, bf16[8,6,64,128]{3,2,1,0:T(8,128)(2,1)S(1)} %collective-permute-done.next_ref), custom_call_target="tpu_custom_call" | custom-call | flops 100663296 | bytes 9175040 | tf_op jit(solution)/shard_map/next_spectra/pallas_call | solution.py:308
Async XLA Ops:
  7.2 37.0 %copy-start.1 = (s32[128]{0:T(128)S(1)}, s32[128]{0:T(128)}, u32[]{:S(2)}) copy-start(s32[128]{0:T(128)} %param.6) | copy-start | bytes 1540
  7.2 37.0 %copy-start.2 = (bf16[1152,1536]{1,0:T(8,128)(2,1)S(1)}, bf16[1152,1536]{1,0:T(8,128)(2,1)}, u32[]{:S(2)}) copy-start(bf16[1152,1536]{1,0:T(8,128)(2,1)} %constant.5.clone.back_ref) | copy-start | bytes 10616836
  49.6 32.9 %copy-start = (s32[128]{0:T(128)S(1)}, s32[128]{0:T(128)}, u32[]{:S(2)}) copy-start(s32[128]{0:T(128)} %param.7) | copy-start | bytes 1540
  78.8 13.3 %collective-permute-start = (bf16[8,6,64,128]{3,2,1,0:T(8,128)(2,1)S(1)}, bf16[8,6,64,128]{3,2,1,0:T(8,128)(2,1)S(1)}, u32[]{:S(2)}, u32[]{:S(2)}) collective-permute-start(bf16[8,6,64,128]{3,2,1,0:T(8,128)(2,1)S(1)} %slice_bitcast_fusion), channel_id=1, source_target_pairs={{8,0},{16,8},{24,16},{32,24},{40,32},{48,40},{56,48},{64,56},{72,6... | collective-permute-start | bytes 2359304 | tf_op jit(solution)/shard_map/ppermute | solution.py:341

commit v4 on v3

--- a/solution.py
+++ b/solution.py
@@ -48,20 +48,23 @@
     return down, back.reshape(2 * BINS, parts * RANK)
 
 
-def project_kernel(down_ref, records_ref, out_ref, held, arrived):
+def project_kernel(down_ref, records_ref, out_ref, held, table, arrived):
     parts, windows = out_ref.shape[:2]
     wide = 4
 
     def fetch(window):
         return pltpu.make_async_copy(records_ref.at[window], held.at[window], arrived.at[window])
 
+    fetch_table = pltpu.make_async_copy(down_ref, table, arrived.at[windows])
+    fetch_table.start()
     for window in range(windows):
         fetch(window).start()
+    fetch_table.wait()
     for window in range(windows):
         fetch(window).wait()
         for start in range(0, parts, wide):
             block = held[window, :, start * LANES : (start + wide) * LANES]
-            both = jnp.dot(down_ref[...], block, preferred_element_type=F32)
+            both = jnp.dot(table[...], block, preferred_element_type=F32)
             sums = (both[:RANK] + both[RANK:]).astype(BF16)
             for part in range(wide):
                 out_ref[start + part, window] = sums[:, part * LANES : (part + 1) * LANES]
@@ -69,19 +72,19 @@
 
 def project(down, records, parts):
     windows, run, channels = records.shape
+    down = pltpu.with_memory_space_constraint(down, pltpu.HBM)
+    records = pltpu.with_memory_space_constraint(records, pltpu.HBM)
     return pl.pallas_call(
         project_kernel,
-        in_specs=[
-            pl.BlockSpec(memory_space=pltpu.VMEM),
-            pl.BlockSpec(memory_space=pltpu.HBM),
-        ],
+        in_specs=[pl.BlockSpec(memory_space=pltpu.HBM)] * 2,
         out_specs=pl.BlockSpec(memory_space=pltpu.VMEM),
         out_shape=jax.ShapeDtypeStruct((parts, windows, RANK, LANES), BF16),
         scratch_shapes=[
             pltpu.VMEM(records.shape, BF16),
-            pltpu.SemaphoreType.DMA((windows,)),
-        ],
-        compiler_params=pltpu.CompilerParams(vmem_limit_bytes=56 * 2**20),
+            pltpu.VMEM(down.shape, BF16),
+            pltpu.SemaphoreType.DMA((windows + 1,)),
+        ],
+        compiler_params=pltpu.CompilerParams(vmem_limit_bytes=24 * 2**20),
         cost_estimate=pl.CostEstimate(
             flops=4 * RANK * run * channels * windows,
             bytes_accessed=2 * records.size + 2 * parts * windows * RANK * LANES,
@@ -95,49 +98,58 @@
     return pltpu.roll(values, values.shape[0] - rows, axis=0)
 
 
-def whiten_kernel(live_ref, back_ref, sums_ref, out_ref):
-    parts = sums_ref.shape[0]
-    columns = jnp.concatenate(
-        [sums_ref[:, i].reshape(parts * RANK, LANES) for i in range(2)], axis=1
-    )
-    spectra = jnp.dot(back_ref[...], columns, preferred_element_type=F32)
-    real_part = spectra[:BINS]
-    imag_part = spectra[BINS:]
-    amplitude = jnp.sqrt(real_part * real_part + imag_part * imag_part)
-    total = amplitude
-    for reach in (1, 2, 4):
-        total = total + up_by(total, reach)
-    for reach in (8, 16, 32):
-        total = total[: total.shape[0] - reach] + total[reach:]
-    smooth = (total[:NB] + amplitude[2 * HALF :]) * (1.0 / (2 * HALF + 1))
+def whiten_kernel(live_ref, back_ref, sums_ref, out_ref, spectra):
+    parts, windows = sums_ref.shape[:2]
+    groups = out_ref.shape[0]
+    rows = 2 * BINS // 3
     live = live_ref[...].astype(F32)
-    scale = jnp.concatenate([live, live], axis=1) / (smooth + 1e-06)
-    real_part = real_part[HALF : HALF + NB] * scale
-    imag_part = imag_part[HALF : HALF + NB] * scale
-    groups = out_ref.shape[0]
+    live = jnp.concatenate([live, live], axis=1)
     left = lax.broadcasted_iota(jnp.int32, (NB, LANES), 1) < LANES // 2
-    for i in range(2):
-        real_one = real_part[:, i * LANES : (i + 1) * LANES]
-        imag_one = imag_part[:, i * LANES : (i + 1) * LANES]
-        first = jnp.where(left, real_one, pltpu.roll(imag_one, LANES // 2, axis=1))
-        second = jnp.where(left, pltpu.roll(real_one, LANES // 2, axis=1), imag_one)
-        out_ref[:, 0, i] = first.astype(BF16).reshape(groups, NB // groups, LANES)
-        out_ref[:, 1, i] = second.astype(BF16).reshape(groups, NB // groups, LANES)
+
+    def transform(pair):
+        columns = jnp.concatenate(
+            [sums_ref[:, 2 * pair + i].reshape(parts * RANK, LANES) for i in range(2)], axis=1
+        )
+        for start in range(0, 2 * BINS, rows):
+            spectra[pair % 2, start : start + rows] = jnp.dot(
+                back_ref[start : start + rows], columns, preferred_element_type=F32
+            )
+
+    transform(0)
+    for pair in range(windows // 2):
+        if 2 * pair + 2 < windows:
+            transform(pair + 1)
+        real_part = spectra[pair % 2, :BINS]
+        imag_part = spectra[pair % 2, BINS:]
+        amplitude = jnp.sqrt(real_part * real_part + imag_part * imag_part)
+        total = amplitude
+        for reach in (8, 16, 32):
+            total = total[: total.shape[0] - reach] + total[reach:]
+        for reach in (1, 2, 4):
+            total = total + up_by(total, reach)
+        smooth = (total[:NB] + amplitude[2 * HALF :]) * (1.0 / (2 * HALF + 1))
+        scale = live / (smooth + 1e-06)
+        real_part = real_part[HALF : HALF + NB] * scale
+        imag_part = imag_part[HALF : HALF + NB] * scale
+        for i in range(2):
+            real_one = real_part[:, i * LANES : (i + 1) * LANES]
+            imag_one = imag_part[:, i * LANES : (i + 1) * LANES]
+            first = jnp.where(left, real_one, pltpu.roll(imag_one, LANES // 2, axis=1))
+            second = jnp.where(left, pltpu.roll(real_one, LANES // 2, axis=1), imag_one)
+            for half, value in enumerate((first, second)):
+                value = value.astype(BF16).reshape(groups, NB // groups, LANES)
+                out_ref[:, half, 2 * pair + i] = value
 
 
 def whiten(live, back, sums, groups):
     parts, windows = sums.shape[:2]
-    shape = (groups, 2, windows, NB // groups, LANES)
+    resident = pl.BlockSpec(memory_space=pltpu.VMEM)
     return pl.pallas_call(
         whiten_kernel,
-        grid=(windows // 2,),
-        in_specs=[
-            pl.BlockSpec((1, LANES), lambda w: (0, 0)),
-            pl.BlockSpec(back.shape, lambda w: (0, 0)),
-            pl.BlockSpec((parts, 2, RANK, LANES), lambda w: (0, w, 0, 0)),
-        ],
-        out_specs=pl.BlockSpec((groups, 2, 2, NB // groups, LANES), lambda w: (0, 0, w, 0, 0)),
-        out_shape=jax.ShapeDtypeStruct(shape, BF16),
+        in_specs=[resident] * 3,
+        out_specs=resident,
+        out_shape=jax.ShapeDtypeStruct((groups, 2, windows, NB // groups, LANES), BF16),
+        scratch_shapes=[pltpu.VMEM((2, 2 * BINS, 2 * LANES), F32)],
         compiler_params=pltpu.CompilerParams(vmem_limit_bytes=28 * 2**20),
         cost_estimate=pl.CostEstimate(
             flops=2 * back.size * windows * LANES,
@@ -245,9 +257,11 @@
 
         def next_part(index):
             after = next_rows[pl.ds(index, every, stride=PITCH), :]
-            partner = jnp.concatenate([after, pltpu.roll(after, half, axis=1)], axis=0)
-            partner = partner.T[:half].astype(BF16)
-            return lowered(jnp.dot(partner, later_ref[base + index], preferred_element_type=F32))
+            partner = after.astype(BF16).T
+            later = later_ref[base + index]
+            gram = jnp.dot(partner[:half], later[:every], preferred_element_type=F32)
+            gram += jnp.dot(partner[half:], later[every:], preferred_element_type=F32)
+            return lowered(gram)
 
         for start in range(0, bins, 8):
             extra = [next_part(start + at) for at in range(8)]

time: 97 us -> 92.3 us (0.952)
  Pallas kernels: 21.2 us -> 16.8 us
    pallas_call x1, Pallas kernels: 7.2 us -> 4.98 us  [project(): pl.pallas_call(project_kernel, in_specs=[pl.BlockSpec(memory_space=pltpu....]
    pallas_call x1, Pallas kernels: 5.4 us -> 4.31 us  [whiten(): pl.pallas_call(whiten_kernel, in_specs=[resident] * 3, out_specs=resident...]
    pallas_call x1, Pallas kernels: 4.64 us -> 3.58 us  [next_spectra(): pl.pallas_call(next_kernel, in_specs=[resident] * 4, out_specs=pl.BlockSp...]
where the time goes in v4:
time: 92.3 us; the launch traced here: 92.2 us
  blocking collectives  65.9 us (71%)
  Pallas kernels  16.8 us (18%)
  waiting for transfers between devices  5.62 us (6%)
  starting transfers between devices  3.76 us (4%)
    all_to_all x2, blocking collectives, exchanged(): flat = lax.all_to_all(flat, axis, split_axis=0, concat_axis=0, tiled=True)  65.9 us
    ppermute x1, waiting for transfers between devices, body(): lax.ppermute(halves[:, 0], 'fibre', [(i, i - 1) for i in range(1, parts)])  5.62 us
    pallas_call x1, Pallas kernels, project(): pl.pallas_call(project_kernel, in_specs=[pl.BlockSpec(memory_space=pltpu....  4.98 us
    pallas_call x1, Pallas kernels, whiten(): pl.pallas_call(whiten_kernel, in_specs=[resident] * 3, out_specs=resident...  4.31 us
    pallas_call x1, Pallas kernels, own_spectra(): pl.pallas_call(own_kernel, grid=(bins // step,), in_specs=[pl.BlockSpec((...  3.93 us
    ppermute x1, starting transfers between devices, body(): lax.ppermute(halves[:, 0], 'fibre', [(i, i - 1) for i in range(1, parts)])  3.76 us
    pallas_call x1, Pallas kernels, next_spectra(): pl.pallas_call(next_kernel, in_specs=[resident] * 4, out_specs=pl.BlockSp...  3.58 us
  transfers between devices with their start and end apart: 1, of which 1 were waited for; matrix products, arithmetic and copies ran while one was open for 0% of the time, Pallas kernels for 4%

profile of v4, /device:TPU:1, one launch (start us, length us, event | category | flops | bytes accessed | tf_op | source)
XLA Modules:
  0.0 92.2 jit_solution(12088371146472999217)
XLA Ops:
  0.0 5.0 %project.1 = bf16[16,6,96,128]{3,2,1,0:T(8,128)(2,1)S(1)} custom-call(bf16[192,375]{1,0:T(8,128)(2,1)} %constant.4.clone.down_ref, bf16[6,375,2048]{2,1,0:T(8,128)(2,1)} %records_ref.1), custom_call_target="tpu_custom_call" | custom-call | flops 1769472000 | bytes 11575296 | tf_op jit(solution)/shard_map/project/pallas_call | solution.py:77
  5.0 0.0 copy-start.1
  5.0 0.0 copy-start.2
  5.0 36.8 %all_to_all.10 = bf16[16,576,128]{2,1,0:T(8,128)(2,1)S(1)} all-to-all(bf16[16,576,128]{2,1,0:T(8,128)(2,1)S(1)} %bitcast.12), channel_id=1, replica_groups=mesh['fibre'=16,'freq'=8] {'fibre'}, dimensions={0} | all-to-all | bytes 4718592 | tf_op jit(solution)/shard_map/all_to_all | solution.py:344
  41.8 0.0 copy-done.1
  41.8 0.0 copy-done.2
  41.8 4.3 %whiten.1 = bf16[8,2,6,64,128]{4,3,2,1,0:T(8,128)(2,1)S(1)} custom-call(s32[1,128]{1,0:T(1,128)S(1)} %bitcast.17, bf16[1152,1536]{1,0:T(8,128)(2,1)S(1)} %copy-done.2, bf16[16,6,96,128]{3,2,1,0:T(8,128)(2,1)S(1)} %bitcast.13), custom_call_target="tpu_custom_call" | custom-call | flops 2717908992 | bytes 7471104 | tf_op jit(solution)/shard_map/whiten/pallas_call | solution.py:147
  46.1 0.0 copy-start
  46.1 29.1 %all_to_all.11 = bf16[8,768,128]{2,1,0:T(8,128)(2,1)S(1)} all-to-all(bf16[8,768,128]{2,1,0:T(8,128)(2,1)S(1)} %bitcast.14), channel_id=1, replica_groups=mesh['fibre'=16,'freq'=8] {'freq'}, dimensions={0} | all-to-all | bytes 3145728 | tf_op jit(solution)/shard_map/all_to_all | solution.py:344
  75.2 0.1 slice_bitcast_fusion
  75.3 3.8 %collective-permute-start = (bf16[8,6,64,128]{3,2,1,0:T(8,128)(2,1)S(1)}, bf16[8,6,64,128]{3,2,1,0:T(8,128)(2,1)S(1)}, u32[]{:S(2)}, u32[]{:S(2)}) collective-permute-start(bf16[8,6,64,128]{3,2,1,0:T(8,128)(2,1)S(1)} %slice_bitcast_fusion), channel_id=1, source_target_pairs={{8,0},{16,8},{24,16},{32,24},{40,32},{48,40},{56,48},{64,56},{72,6... | collective-permute-start | bytes 2359304 | tf_op jit(solution)/shard_map/ppermute | solution.py:355
  79.0 0.0 copy-done
  79.0 3.9 %own_spectra.1 = (f32[64,2,64,128]{3,2,1,0:T(8,128)S(1)}, bf16[64,96,128]{2,1,0:T(8,128)(2,1)S(1)}) custom-call(s32[1,128]{1,0:T(1,128)S(1)} %bitcast.15, bf16[8,2,6,64,128]{4,3,2,1,0:T(8,128)(2,1)S(1)} %bitcast.11), custom_call_target="tpu_custom_call" | custom-call | flops 402653184 | bytes 7340032 | tf_op jit(solution)/shard_map/own_spectra/pallas_call | solution.py:291
  83.0 5.6 %collective-permute-done.next_ref = bf16[8,6,64,128]{3,2,1,0:T(8,128)(2,1)S(1)} collective-permute-done((bf16[8,6,64,128]{3,2,1,0:T(8,128)(2,1)S(1)}, bf16[8,6,64,128]{3,2,1,0:T(8,128)(2,1)S(1)}, u32[]{:S(2)}, u32[]{:S(2)}) %collective-permute-start) | collective-permute-done | bytes 786464 | tf_op jit(solution)/shard_map/ppermute | solution.py:355
  88.6 3.6 %next_spectra.1 = f32[64,2,64,128]{3,2,1,0:T(8,128)} custom-call(s32[1,128]{1,0:T(1,128)S(1)} %bitcast.16, f32[64,2,64,128]{3,2,1,0:T(8,128)S(1)} %get-tuple-element.7.part_ref, bf16[64,96,128]{2,1,0:T(8,128)(2,1)S(1)} %get-tuple-element.8.later_ref, bf16[8,6,64,128]{3,2,1,0:T(8,128)(2,1)S(1)} %collective-permute-done.next_ref), custom_call_target="tpu_custom_call" | custom-call | flops 100663296 | bytes 9175040 | tf_op jit(solution)/shard_map/next_spectra/pallas_call | solution.py:322
Async XLA Ops:
  5.0 36.8 %copy-start.1 = (s32[128]{0:T(128)S(1)}, s32[128]{0:T(128)}, u32[]{:S(2)}) copy-start(s32[128]{0:T(128)} %param.6) | copy-start | bytes 1540
  5.0 36.8 %copy-start.2 = (bf16[1152,1536]{1,0:T(8,128)(2,1)S(1)}, bf16[1152,1536]{1,0:T(8,128)(2,1)}, u32[]{:S(2)}) copy-start(bf16[1152,1536]{1,0:T(8,128)(2,1)} %constant.5.clone.back_ref) | copy-start | bytes 10616836
  46.1 32.9 %copy-start = (s32[128]{0:T(128)S(1)}, s32[128]{0:T(128)}, u32[]{:S(2)}) copy-start(s32[128]{0:T(128)} %param.7) | copy-start | bytes 1540
  75.3 13.3 %collective-permute-start = (bf16[8,6,64,128]{3,2,1,0:T(8,128)(2,1)S(1)}, bf16[8,6,64,128]{3,2,1,0:T(8,128)(2,1)S(1)}, u32[]{:S(2)}, u32[]{:S(2)}) collective-permute-start(bf16[8,6,64,128]{3,2,1,0:T(8,128)(2,1)S(1)} %slice_bitcast_fusion), channel_id=1, source_target_pairs={{8,0},{16,8},{24,16},{32,24},{40,32},{48,40},{56,48},{64,56},{72,6... | collective-permute-start | bytes 2359304 | tf_op jit(solution)/shard_map/ppermute | solution.py:355

commit v5 on v4

--- a/solution.py
+++ b/solution.py
@@ -220,9 +220,10 @@
         later_ref[pl.ds(index, 1)] = late.astype(BF16)[None]
 
 
-def next_kernel(limit_ref, part_ref, later_ref, next_ref, out_ref, next_all, held, sent):
+def next_kernel(begin, limit_ref, part_ref, later_ref, next_ref, *refs):
+    out_ref, next_all, held, sent = refs[-4:]
     groups, windows, _, _ = next_ref.shape
-    steps, bins = held.shape[0], held.shape[3]
+    steps, bins = held.shape[0] // 2, 16
     every = groups * windows
     half = LANES // 2
     lane = lax.broadcasted_iota(jnp.int32, (half, LANES), 1)
@@ -245,13 +246,13 @@
     keep = ((offsets <= limit_ref[...]) & (lanes >= half)).astype(F32)
 
     def send(step):
-        where = pl.ds(pl.multiple_of(step * bins, bins), bins)
+        where = pl.ds(pl.multiple_of(begin + step * 8, 8), 8)
         return pltpu.make_async_copy(held.at[step], out_ref.at[:, :, where], sent.at[step])
 
     @pl.loop(0, steps)
     def _(step):
-        base = pl.multiple_of(step * bins, bins)
-        after_all = next_ref[:, :, pl.ds(base, bins)]
+        base = begin + step * bins
+        after_all = next_ref[:, :, pl.ds(pl.multiple_of(step * bins, bins), bins)]
         next_all[:, :bins] = after_all.astype(F32).reshape(every, bins, LANES)
         next_rows = next_all.reshape(every * PITCH, LANES)
 
@@ -276,10 +277,10 @@
                         own = part_ref[base + start + at, part, tile : tile + 8]
                         sums.append(own + value)
                     for at, value in enumerate(swapped(sums)):
-                        held[step, tile + at, part, start : start + 8] = value
-        send(step).start()
-
-    for step in range(steps):
+                        held[2 * step + start // 8, tile + at, part] = value
+            send(2 * step + start // 8).start()
+
+    for step in range(2 * steps):
         send(step).wait()
 
 
@@ -314,20 +315,23 @@
     )(limit, halves)
 
 
-def next_spectra(limit, own, later, after):
+def next_spectra(limit, own, later, after, begin, done):
     groups, windows, bins, _ = after.shape
     step = 16
     every = groups * windows
     resident = pl.BlockSpec(memory_space=pltpu.VMEM)
+    anywhere = pl.BlockSpec(memory_space=pl.ANY)
+    filled = [] if done is None else [done]
     return pl.pallas_call(
-        next_kernel,
-        in_specs=[resident] * 4,
-        out_specs=pl.BlockSpec(memory_space=pl.ANY),
-        out_shape=jax.ShapeDtypeStruct((OFFSETS, 2, bins, LANES), F32),
+        functools.partial(next_kernel, begin),
+        in_specs=[resident] * 4 + [anywhere] * len(filled),
+        out_specs=anywhere,
+        out_shape=jax.ShapeDtypeStruct((OFFSETS, 2, own.shape[0], LANES), F32),
+        input_output_aliases={4: 0} if filled else {},
         scratch_shapes=[
             pltpu.VMEM((every, PITCH, LANES), F32),
-            pltpu.VMEM((bins // step, OFFSETS, 2, step, LANES), F32),
-            pltpu.SemaphoreType.DMA((bins // step,)),
+            pltpu.VMEM((bins // 8, OFFSETS, 2, 8, LANES), F32),
+            pltpu.SemaphoreType.DMA((bins // 8,)),
         ],
         compiler_params=pltpu.CompilerParams(vmem_limit_bytes=20 * 2**20),
         cost_estimate=pl.CostEstimate(
@@ -336,7 +340,7 @@
             transcendentals=0,
         ),
         name="next_spectra",
-    )(limit, own, later, after)
+    )(limit, own, later, after, *filled)
 
 
 def exchanged(blocks, axis):
@@ -352,9 +356,18 @@
     sums = exchanged(sums, "fibre")
     halves = whiten(channel_live[None, :], back, sums, groups)
     halves = exchanged(halves, "freq")
-    after = lax.ppermute(halves[:, 0], "fibre", [(i, i - 1) for i in range(1, parts)])
-    own, later = own_spectra(offset_limit[None, :], halves)
-    return next_spectra(offset_limit[None, :], own, later, after)
+    back_one = [(i, i - 1) for i in range(1, parts)]
+    bounds = (0, 32, NB // groups)
+    after = [
+        lax.ppermute(halves[:, 0, :, low:high], "fibre", back_one)
+        for low, high in zip(bounds, bounds[1:])
+    ]
+    limit = offset_limit[None, :]
+    own, later = own_spectra(limit, halves)
+    out = None
+    for low, piece in zip(bounds, after):
+        out = next_spectra(limit, own, later, piece, low, out)
+    return out
 
 
 def solution(mesh):

time: 92.3 us -> 91 us (0.986)
  waiting for transfers between devices: 5.62 us -> 1.5 us
  starting transfers between devices: 3.76 us -> 5.68 us
    ppermute x1 -> x2, waiting for transfers between devices: 5.62 us -> 1.5 us  [body(): lax.ppermute(halves[:, 0, :, low:high], 'fibre', back_one)]
    ppermute x1 -> x2, starting transfers between devices: 3.76 us -> 5.68 us  [body(): lax.ppermute(halves[:, 0, :, low:high], 'fibre', back_one)]
    pallas_call x1 -> x2, Pallas kernels: 3.58 us -> 4.36 us  [next_spectra(): pl.pallas_call(functools.partial(next_kernel, begin), in_specs=[resident]...]
  transfers between devices with their start and end apart: 1 -> 2, of which waited for: 1 -> 1; matrix products, arithmetic and copies ran while one was open for 0% -> 0% of each run, Pallas kernels for 4% -> 7%
where the time goes in v5:
time: 91 us; the launch traced here: 90.8 us
  blocking collectives  65.9 us (72%)
  Pallas kernels  17.6 us (19%)
  starting transfers between devices  5.68 us (6%)
  waiting for transfers between devices  1.5 us (2%)
    all_to_all x2, blocking collectives, exchanged(): flat = lax.all_to_all(flat, axis, split_axis=0, concat_axis=0, tiled=True)  65.9 us
    ppermute x2, starting transfers between devices, body(): lax.ppermute(halves[:, 0, :, low:high], 'fibre', back_one)  5.68 us
    pallas_call x1, Pallas kernels, project(): pl.pallas_call(project_kernel, in_specs=[pl.BlockSpec(memory_space=pltpu....  4.98 us
    pallas_call x2, Pallas kernels, next_spectra(): pl.pallas_call(functools.partial(next_kernel, begin), in_specs=[resident]...  4.36 us
    pallas_call x1, Pallas kernels, whiten(): pl.pallas_call(whiten_kernel, in_specs=[resident] * 3, out_specs=resident...  4.31 us
    pallas_call x1, Pallas kernels, own_spectra(): pl.pallas_call(own_kernel, grid=(bins // step,), in_specs=[pl.BlockSpec((...  3.93 us
  transfers between devices with their start and end apart: 2, of which 1 were waited for; matrix products, arithmetic and copies ran while one was open for 0% of the time, Pallas kernels for 7%

profile of v5, /device:TPU:1, one launch (start us, length us, event | category | flops | bytes accessed | tf_op | source)
XLA Modules:
  0.0 90.8 jit_solution(13227866236476710481)
XLA Ops:
  0.0 5.0 %project.1 = bf16[16,6,96,128]{3,2,1,0:T(8,128)(2,1)S(1)} custom-call(bf16[192,375]{1,0:T(8,128)(2,1)} %constant.4.clone.down_ref, bf16[6,375,2048]{2,1,0:T(8,128)(2,1)} %records_ref.1), custom_call_target="tpu_custom_call" | custom-call | flops 1769472000 | bytes 11575296 | tf_op jit(solution)/shard_map/project/pallas_call | solution.py:77
  5.0 0.0 copy-start.1
  5.0 0.0 copy-start.2
  5.0 36.8 %all_to_all.10 = bf16[16,576,128]{2,1,0:T(8,128)(2,1)S(1)} all-to-all(bf16[16,576,128]{2,1,0:T(8,128)(2,1)S(1)} %bitcast.16), channel_id=1, replica_groups=mesh['fibre'=16,'freq'=8] {'fibre'}, dimensions={0} | all-to-all | bytes 4718592 | tf_op jit(solution)/shard_map/all_to_all | solution.py:348
  41.8 0.0 copy-done.1
  41.8 0.0 copy-done.2
  41.8 4.3 %whiten.1 = bf16[8,2,6,64,128]{4,3,2,1,0:T(8,128)(2,1)S(1)} custom-call(s32[1,128]{1,0:T(1,128)S(1)} %bitcast.22, bf16[1152,1536]{1,0:T(8,128)(2,1)S(1)} %copy-done.2, bf16[16,6,96,128]{3,2,1,0:T(8,128)(2,1)S(1)} %bitcast.17), custom_call_target="tpu_custom_call" | custom-call | flops 2717908992 | bytes 7471104 | tf_op jit(solution)/shard_map/whiten/pallas_call | solution.py:147
  46.1 0.0 copy-start
  46.1 29.1 %all_to_all.11 = bf16[8,768,128]{2,1,0:T(8,128)(2,1)S(1)} all-to-all(bf16[8,768,128]{2,1,0:T(8,128)(2,1)S(1)} %bitcast.18), channel_id=1, replica_groups=mesh['fibre'=16,'freq'=8] {'freq'}, dimensions={0} | all-to-all | bytes 3145728 | tf_op jit(solution)/shard_map/all_to_all | solution.py:348
  75.2 0.1 slice_bitcast_fusion
  75.3 3.8 %collective-permute-start.1 = (bf16[8,6,32,128]{3,2,1,0:T(8,128)(2,1)S(1)}, bf16[8,6,32,128]{3,2,1,0:T(8,128)(2,1)S(1)}, u32[]{:S(2)}, u32[]{:S(2)}) collective-permute-start(bf16[8,6,32,128]{3,2,1,0:T(8,128)(2,1)S(1)} %get-tuple-element.9), channel_id=1, source_target_pairs={{8,0},{16,8},{24,16},{32,24},{40,32},{48,40},{56,48},{64,56},{72,6... | collective-permute-start | bytes 1179656 | tf_op jit(solution)/shard_map/ppermute | solution.py:362
  79.0 1.9 %collective-permute-start = (bf16[8,6,32,128]{3,2,1,0:T(8,128)(2,1)S(1)}, bf16[8,6,32,128]{3,2,1,0:T(8,128)(2,1)S(1)}, u32[]{:S(2)}, u32[]{:S(2)}) collective-permute-start(bf16[8,6,32,128]{3,2,1,0:T(8,128)(2,1)S(1)} %get-tuple-element.10), channel_id=1, source_target_pairs={{8,0},{16,8},{24,16},{32,24},{40,32},{48,40},{56,48},{64,56},{72,6... | collective-permute-start | bytes 1179656 | tf_op jit(solution)/shard_map/ppermute | solution.py:362
  81.0 0.0 copy-done
  81.0 3.9 %own_spectra.1 = (f32[64,2,64,128]{3,2,1,0:T(8,128)S(1)}, bf16[64,96,128]{2,1,0:T(8,128)(2,1)S(1)}) custom-call(s32[1,128]{1,0:T(1,128)S(1)} %bitcast.19, bf16[8,2,6,64,128]{4,3,2,1,0:T(8,128)(2,1)S(1)} %bitcast.15), custom_call_target="tpu_custom_call" | custom-call | flops 402653184 | bytes 7340032 | tf_op jit(solution)/shard_map/own_spectra/pallas_call | solution.py:292
  84.9 0.0 collective-permute-done.1.next_ref
  84.9 2.2 %next_spectra.2.refs_0_ = f32[64,2,64,128]{3,2,1,0:T(8,128)} custom-call(s32[1,128]{1,0:T(1,128)S(1)} %bitcast.20, f32[64,2,64,128]{3,2,1,0:T(8,128)S(1)} %get-tuple-element.7.part_ref, bf16[64,96,128]{2,1,0:T(8,128)(2,1)S(1)} %get-tuple-element.8.later_ref, bf16[8,6,32,128]{3,2,1,0:T(8,128)(2,1)S(1)} %collective-permute-done.1.next_ref), custom_call_target="tpu_custom_call" | custom-call | flops 50331648 | bytes 4587520 | tf_op jit(solution)/shard_map/next_spectra/pallas_call | solution.py:325
  87.1 1.5 %collective-permute-done.next_ref = bf16[8,6,32,128]{3,2,1,0:T(8,128)(2,1)S(1)} collective-permute-done((bf16[8,6,32,128]{3,2,1,0:T(8,128)(2,1)S(1)}, bf16[8,6,32,128]{3,2,1,0:T(8,128)(2,1)S(1)}, u32[]{:S(2)}, u32[]{:S(2)}) %collective-permute-start) | collective-permute-done | bytes 393248 | tf_op jit(solution)/shard_map/ppermute | solution.py:362
  88.6 2.2 %next_spectra.3 = f32[64,2,64,128]{3,2,1,0:T(8,128)} custom-call(s32[1,128]{1,0:T(1,128)S(1)} %bitcast.21, f32[64,2,64,128]{3,2,1,0:T(8,128)S(1)} %get-tuple-element.7.part_ref, bf16[64,96,128]{2,1,0:T(8,128)(2,1)S(1)} %get-tuple-element.8.later_ref, bf16[8,6,32,128]{3,2,1,0:T(8,128)(2,1)S(1)} %collective-permute-done.next_ref, ...), custom_call_target="tpu_custom_call", output_to_operand_aliasing={{}: (4, {})} | custom-call | flops 50331648 | bytes 4587520 | tf_op jit(solution)/shard_map/next_spectra/pallas_call | solution.py:325
Async XLA Ops:
  5.0 36.8 %copy-start.1 = (s32[128]{0:T(128)S(1)}, s32[128]{0:T(128)}, u32[]{:S(2)}) copy-start(s32[128]{0:T(128)} %param.6) | copy-start | bytes 1540
  5.0 36.8 %copy-start.2 = (bf16[1152,1536]{1,0:T(8,128)(2,1)S(1)}, bf16[1152,1536]{1,0:T(8,128)(2,1)}, u32[]{:S(2)}) copy-start(bf16[1152,1536]{1,0:T(8,128)(2,1)} %constant.5.clone.back_ref) | copy-start | bytes 10616836
  46.1 34.9 %copy-start = (s32[128]{0:T(128)S(1)}, s32[128]{0:T(128)}, u32[]{:S(2)}) copy-start(s32[128]{0:T(128)} %param.7) | copy-start | bytes 1540
  75.3 9.6 %collective-permute-start.1 = (bf16[8,6,32,128]{3,2,1,0:T(8,128)(2,1)S(1)}, bf16[8,6,32,128]{3,2,1,0:T(8,128)(2,1)S(1)}, u32[]{:S(2)}, u32[]{:S(2)}) collective-permute-start(bf16[8,6,32,128]{3,2,1,0:T(8,128)(2,1)S(1)} %get-tuple-element.9), channel_id=1, source_target_pairs={{8,0},{16,8},{24,16},{32,24},{40,32},{48,40},{56,48},{64,56},{72,6... | collective-permute-start | bytes 1179656 | tf_op jit(solution)/shard_map/ppermute | solution.py:362
  79.0 9.6 %collective-permute-start = (bf16[8,6,32,128]{3,2,1,0:T(8,128)(2,1)S(1)}, bf16[8,6,32,128]{3,2,1,0:T(8,128)(2,1)S(1)}, u32[]{:S(2)}, u32[]{:S(2)}) collective-permute-start(bf16[8,6,32,128]{3,2,1,0:T(8,128)(2,1)S(1)} %get-tuple-element.10), channel_id=1, source_target_pairs={{8,0},{16,8},{24,16},{32,24},{40,32},{48,40},{56,48},{64,56},{72,6... | collective-permute-start | bytes 1179656 | tf_op jit(solution)/shard_map/ppermute | solution.py:362

commit v6 on v5

--- a/solution.py
+++ b/solution.py
@@ -170,13 +170,11 @@
 
 
 def own_kernel(limit_ref, halves_ref, part_ref, later_ref, first_all, second_all):
-    groups, _, windows, bins, _ = halves_ref.shape
+    groups, _, windows, _, _ = halves_ref.shape
+    bins = 16
+    steps = halves_ref.shape[3] // bins
     every = groups * windows
     half = LANES // 2
-    first_all[:, :bins] = halves_ref[:, 0].astype(F32).reshape(every, bins, LANES)
-    second_all[:, :bins] = halves_ref[:, 1].astype(F32).reshape(every, bins, LANES)
-    first_rows = first_all.reshape(every * PITCH, LANES)
-    second_rows = second_all.reshape(every * PITCH, LANES)
     left = lax.broadcasted_iota(jnp.int32, (every, LANES), 1) < half
     offsets = lax.broadcasted_iota(jnp.int32, (OFFSETS, LANES), 0) + 1
     keep = (offsets <= limit_ref[...]).astype(F32)
@@ -196,28 +194,35 @@
         merged = [jnp.where(spot < 8, pieces[p], pieces[p + 1]) for p in range(OFFSETS // 8)]
         return jnp.concatenate(merged, axis=0)
 
-    @pl.loop(0, bins, unroll=16)
-    def _(index):
-        rows = pl.ds(index, every, stride=PITCH)
-        first = first_rows[rows, :]
-        second = second_rows[rows, :]
-        turned = pltpu.roll(second, half, axis=1)
-        real_x = jnp.where(left, first, turned)
-        imag_x = jnp.where(left, pltpu.roll(first, half, axis=1), second)
-        partner = jnp.concatenate([real_x, imag_x], axis=0).T.astype(BF16)
-        own = jnp.concatenate(
-            [
-                jnp.concatenate([real_x, imag_x], axis=1),
-                jnp.concatenate([imag_x, -real_x], axis=1),
-            ],
-            axis=0,
-        ).astype(BF16)
-        gram = jnp.dot(partner, own, preferred_element_type=F32)
-        for part in range(2):
-            value = skewed(gram[:, part * LANES : (part + 1) * LANES]) * keep
-            part_ref[pl.ds(index, 1), part] = value[None]
-        late = jnp.concatenate([second, jnp.where(left, turned, -turned)], axis=0)
-        later_ref[pl.ds(index, 1)] = late.astype(BF16)[None]
+    @pl.loop(0, steps)
+    def _(step):
+        base = pl.multiple_of(step * bins, bins)
+        for half_at, kept in ((0, first_all), (1, second_all)):
+            values = halves_ref[:, half_at, :, pl.ds(base, bins)].astype(F32)
+            values = values.reshape(every, bins, LANES)
+            for row in range(every):
+                kept[row * PITCH : row * PITCH + bins] = values[row]
+        for index in range(bins):
+            rows = pl.ds(index, every, stride=PITCH)
+            first = first_all[rows, :]
+            second = second_all[rows, :]
+            turned = pltpu.roll(second, half, axis=1)
+            real_x = jnp.where(left, first, turned)
+            imag_x = jnp.where(left, pltpu.roll(first, half, axis=1), second)
+            partner = jnp.concatenate([real_x, imag_x], axis=0).T.astype(BF16)
+            own = jnp.concatenate(
+                [
+                    jnp.concatenate([real_x, imag_x], axis=1),
+                    jnp.concatenate([imag_x, -real_x], axis=1),
+                ],
+                axis=0,
+            ).astype(BF16)
+            gram = jnp.dot(partner, own, preferred_element_type=F32)
+            for part in range(2):
+                value = skewed(gram[:, part * LANES : (part + 1) * LANES]) * keep
+                part_ref[base + index, part] = value
+            late = jnp.concatenate([second, jnp.where(left, turned, -turned)], axis=0)
+            later_ref[base + index] = late.astype(BF16)
 
 
 def next_kernel(begin, limit_ref, part_ref, later_ref, next_ref, *refs):
@@ -253,11 +258,12 @@
     def _(step):
         base = begin + step * bins
         after_all = next_ref[:, :, pl.ds(pl.multiple_of(step * bins, bins), bins)]
-        next_all[:, :bins] = after_all.astype(F32).reshape(every, bins, LANES)
-        next_rows = next_all.reshape(every * PITCH, LANES)
+        values = after_all.astype(F32).reshape(every, bins, LANES)
+        for row in range(every):
+            next_all[row * PITCH : row * PITCH + bins] = values[row]
 
         def next_part(index):
-            after = next_rows[pl.ds(index, every, stride=PITCH), :]
+            after = next_all[pl.ds(index, every, stride=PITCH), :]
             partner = after.astype(BF16).T
             later = later_ref[base + index]
             gram = jnp.dot(partner[:half], later[:every], preferred_element_type=F32)
@@ -286,25 +292,17 @@
 
 def own_spectra(limit, halves):
     groups, _, windows, bins, _ = halves.shape
-    step = 16
     every = groups * windows
-    scratch = pltpu.VMEM((every, PITCH, LANES), F32)
+    resident = pl.BlockSpec(memory_space=pltpu.VMEM)
     return pl.pallas_call(
         own_kernel,
-        grid=(bins // step,),
-        in_specs=[
-            pl.BlockSpec((1, LANES), lambda b: (0, 0)),
-            pl.BlockSpec((groups, 2, windows, step, LANES), lambda b: (0, 0, 0, b, 0)),
-        ],
-        out_specs=[
-            pl.BlockSpec((step, 2, OFFSETS, LANES), lambda b: (b, 0, 0, 0)),
-            pl.BlockSpec((step, 2 * every, LANES), lambda b: (b, 0, 0)),
-        ],
+        in_specs=[resident] * 2,
+        out_specs=[resident] * 2,
         out_shape=[
             jax.ShapeDtypeStruct((bins, 2, OFFSETS, LANES), F32),
             jax.ShapeDtypeStruct((bins, 2 * every, LANES), BF16),
         ],
-        scratch_shapes=[scratch] * 2,
+        scratch_shapes=[pltpu.VMEM(((every + 1) * PITCH, LANES), F32)] * 2,
         compiler_params=pltpu.CompilerParams(vmem_limit_bytes=20 * 2**20),
         cost_estimate=pl.CostEstimate(
             flops=2 * bins * 128 * 96 * 256,
@@ -329,7 +327,7 @@
         out_shape=jax.ShapeDtypeStruct((OFFSETS, 2, own.shape[0], LANES), F32),
         input_output_aliases={4: 0} if filled else {},
         scratch_shapes=[
-            pltpu.VMEM((every, PITCH, LANES), F32),
+            pltpu.VMEM(((every + 1) * PITCH, LANES), F32),
             pltpu.VMEM((bins // 8, OFFSETS, 2, 8, LANES), F32),
             pltpu.SemaphoreType.DMA((bins // 8,)),
         ],

time: 91 us -> 91 us (level)
  transfers between devices with their start and end apart: 2 -> 2, of which waited for: 1 -> 1; matrix products, arithmetic and copies ran while one was open for 0% -> 0% of each run, Pallas kernels for 7% -> 6%
where the time goes in v6:
time: 91 us; the launch traced here: 90.8 us
  blocking collectives  65.9 us (72%)
  Pallas kernels  17.4 us (19%)
  starting transfers between devices  5.68 us (6%)
  waiting for transfers between devices  1.72 us (2%)
    all_to_all x2, blocking collectives, exchanged(): flat = lax.all_to_all(flat, axis, split_axis=0, concat_axis=0, tiled=True)  65.9 us
    ppermute x2, starting transfers between devices, body(): lax.ppermute(halves[:, 0, :, low:high], 'fibre', back_one)  5.68 us
    pallas_call x1, Pallas kernels, project(): pl.pallas_call(project_kernel, in_specs=[pl.BlockSpec(memory_space=pltpu....  4.98 us
    pallas_call x2, Pallas kernels, next_spectra(): pl.pallas_call(functools.partial(next_kernel, begin), in_specs=[resident]...  4.35 us
    pallas_call x1, Pallas kernels, whiten(): pl.pallas_call(whiten_kernel, in_specs=[resident] * 3, out_specs=resident...  4.31 us
    pallas_call x1, Pallas kernels, own_spectra(): pl.pallas_call(own_kernel, in_specs=[resident] * 2, out_specs=[resident]...  3.71 us
  transfers between devices with their start and end apart: 2, of which 1 were waited for; matrix products, arithmetic and copies ran while one was open for 0% of the time, Pallas kernels for 6%

profile of v6, /device:TPU:1, one launch (start us, length us, event | category | flops | bytes accessed | tf_op | source)
XLA Modules:
  0.0 90.8 jit_solution(16132010729886518975)
XLA Ops:
  0.0 5.0 %project.1 = bf16[16,6,96,128]{3,2,1,0:T(8,128)(2,1)S(1)} custom-call(bf16[192,375]{1,0:T(8,128)(2,1)} %constant.4.clone.down_ref, bf16[6,375,2048]{2,1,0:T(8,128)(2,1)} %records_ref.1), custom_call_target="tpu_custom_call" | custom-call | flops 1769472000 | bytes 11575296 | tf_op jit(solution)/shard_map/project/pallas_call | solution.py:77
  5.0 0.0 copy-start.1
  5.0 0.0 copy-start.2
  5.0 36.8 %all_to_all.10 = bf16[16,576,128]{2,1,0:T(8,128)(2,1)S(1)} all-to-all(bf16[16,576,128]{2,1,0:T(8,128)(2,1)S(1)} %bitcast.16), channel_id=1, replica_groups=mesh['fibre'=16,'freq'=8] {'fibre'}, dimensions={0} | all-to-all | bytes 4718592 | tf_op jit(solution)/shard_map/all_to_all | solution.py:346
  41.8 0.0 copy-done.1
  41.8 0.0 copy-done.2
  41.8 4.3 %whiten.1 = bf16[8,2,6,64,128]{4,3,2,1,0:T(8,128)(2,1)S(1)} custom-call(s32[1,128]{1,0:T(1,128)S(1)} %bitcast.22, bf16[1152,1536]{1,0:T(8,128)(2,1)S(1)} %copy-done.2, bf16[16,6,96,128]{3,2,1,0:T(8,128)(2,1)S(1)} %bitcast.17), custom_call_target="tpu_custom_call" | custom-call | flops 2717908992 | bytes 7471104 | tf_op jit(solution)/shard_map/whiten/pallas_call | solution.py:147
  46.1 0.0 copy-start
  46.1 29.1 %all_to_all.11 = bf16[8,768,128]{2,1,0:T(8,128)(2,1)S(1)} all-to-all(bf16[8,768,128]{2,1,0:T(8,128)(2,1)S(1)} %bitcast.18), channel_id=1, replica_groups=mesh['fibre'=16,'freq'=8] {'freq'}, dimensions={0} | all-to-all | bytes 3145728 | tf_op jit(solution)/shard_map/all_to_all | solution.py:346
  75.2 0.1 slice_bitcast_fusion
  75.3 3.8 %collective-permute-start.1 = (bf16[8,6,32,128]{3,2,1,0:T(8,128)(2,1)S(1)}, bf16[8,6,32,128]{3,2,1,0:T(8,128)(2,1)S(1)}, u32[]{:S(2)}, u32[]{:S(2)}) collective-permute-start(bf16[8,6,32,128]{3,2,1,0:T(8,128)(2,1)S(1)} %get-tuple-element.9), channel_id=1, source_target_pairs={{8,0},{16,8},{24,16},{32,24},{40,32},{48,40},{56,48},{64,56},{72,6... | collective-permute-start | bytes 1179656 | tf_op jit(solution)/shard_map/ppermute | solution.py:360
  79.0 1.9 %collective-permute-start = (bf16[8,6,32,128]{3,2,1,0:T(8,128)(2,1)S(1)}, bf16[8,6,32,128]{3,2,1,0:T(8,128)(2,1)S(1)}, u32[]{:S(2)}, u32[]{:S(2)}) collective-permute-start(bf16[8,6,32,128]{3,2,1,0:T(8,128)(2,1)S(1)} %get-tuple-element.10), channel_id=1, source_target_pairs={{8,0},{16,8},{24,16},{32,24},{40,32},{48,40},{56,48},{64,56},{72,6... | collective-permute-start | bytes 1179656 | tf_op jit(solution)/shard_map/ppermute | solution.py:360
  81.0 0.0 copy-done
  81.0 3.7 %own_spectra.1 = (f32[64,2,64,128]{3,2,1,0:T(8,128)S(1)}, bf16[64,96,128]{2,1,0:T(8,128)(2,1)S(1)}) custom-call(s32[1,128]{1,0:T(1,128)S(1)} %bitcast.19, bf16[8,2,6,64,128]{4,3,2,1,0:T(8,128)(2,1)S(1)} %bitcast.15), custom_call_target="tpu_custom_call" | custom-call | flops 402653184 | bytes 7340032 | tf_op jit(solution)/shard_map/own_spectra/pallas_call | solution.py:297
  84.7 0.0 collective-permute-done.1.next_ref
  84.7 2.2 %next_spectra.2.refs_0_ = f32[64,2,64,128]{3,2,1,0:T(8,128)} custom-call(s32[1,128]{1,0:T(1,128)S(1)} %bitcast.20, f32[64,2,64,128]{3,2,1,0:T(8,128)S(1)} %get-tuple-element.7.part_ref, bf16[64,96,128]{2,1,0:T(8,128)(2,1)S(1)} %get-tuple-element.8.later_ref, bf16[8,6,32,128]{3,2,1,0:T(8,128)(2,1)S(1)} %collective-permute-done.1.next_ref), custom_call_target="tpu_custom_call" | custom-call | flops 50331648 | bytes 4587520 | tf_op jit(solution)/shard_map/next_spectra/pallas_call | solution.py:323
  86.9 1.7 %collective-permute-done.next_ref = bf16[8,6,32,128]{3,2,1,0:T(8,128)(2,1)S(1)} collective-permute-done((bf16[8,6,32,128]{3,2,1,0:T(8,128)(2,1)S(1)}, bf16[8,6,32,128]{3,2,1,0:T(8,128)(2,1)S(1)}, u32[]{:S(2)}, u32[]{:S(2)}) %collective-permute-start) | collective-permute-done | bytes 393248 | tf_op jit(solution)/shard_map/ppermute | solution.py:360
  88.6 2.2 %next_spectra.3 = f32[64,2,64,128]{3,2,1,0:T(8,128)} custom-call(s32[1,128]{1,0:T(1,128)S(1)} %bitcast.21, f32[64,2,64,128]{3,2,1,0:T(8,128)S(1)} %get-tuple-element.7.part_ref, bf16[64,96,128]{2,1,0:T(8,128)(2,1)S(1)} %get-tuple-element.8.later_ref, bf16[8,6,32,128]{3,2,1,0:T(8,128)(2,1)S(1)} %collective-permute-done.next_ref, ...), custom_call_target="tpu_custom_call", output_to_operand_aliasing={{}: (4, {})} | custom-call | flops 50331648 | bytes 4587520 | tf_op jit(solution)/shard_map/next_spectra/pallas_call | solution.py:323
Async XLA Ops:
  5.0 36.8 %copy-start.1 = (s32[128]{0:T(128)S(1)}, s32[128]{0:T(128)}, u32[]{:S(2)}) copy-start(s32[128]{0:T(128)} %param.6) | copy-start | bytes 1540
  5.0 36.8 %copy-start.2 = (bf16[1152,1536]{1,0:T(8,128)(2,1)S(1)}, bf16[1152,1536]{1,0:T(8,128)(2,1)}, u32[]{:S(2)}) copy-start(bf16[1152,1536]{1,0:T(8,128)(2,1)} %constant.5.clone.back_ref) | copy-start | bytes 10616836
  46.1 34.9 %copy-start = (s32[128]{0:T(128)S(1)}, s32[128]{0:T(128)}, u32[]{:S(2)}) copy-start(s32[128]{0:T(128)} %param.7) | copy-start | bytes 1540
  75.3 9.4 %collective-permute-start.1 = (bf16[8,6,32,128]{3,2,1,0:T(8,128)(2,1)S(1)}, bf16[8,6,32,128]{3,2,1,0:T(8,128)(2,1)S(1)}, u32[]{:S(2)}, u32[]{:S(2)}) collective-permute-start(bf16[8,6,32,128]{3,2,1,0:T(8,128)(2,1)S(1)} %get-tuple-element.9), channel_id=1, source_target_pairs={{8,0},{16,8},{24,16},{32,24},{40,32},{48,40},{56,48},{64,56},{72,6... | collective-permute-start | bytes 1179656 | tf_op jit(solution)/shard_map/ppermute | solution.py:360
  79.0 9.6 %collective-permute-start = (bf16[8,6,32,128]{3,2,1,0:T(8,128)(2,1)S(1)}, bf16[8,6,32,128]{3,2,1,0:T(8,128)(2,1)S(1)}, u32[]{:S(2)}, u32[]{:S(2)}) collective-permute-start(bf16[8,6,32,128]{3,2,1,0:T(8,128)(2,1)S(1)} %get-tuple-element.10), channel_id=1, source_target_pairs={{8,0},{16,8},{24,16},{32,24},{40,32},{48,40},{56,48},{64,56},{72,6... | collective-permute-start | bytes 1179656 | tf_op jit(solution)/shard_map/ppermute | solution.py:360

commit v7 on v6

--- a/solution.py
+++ b/solution.py
@@ -101,7 +101,7 @@
 def whiten_kernel(live_ref, back_ref, sums_ref, out_ref, spectra):
     parts, windows = sums_ref.shape[:2]
     groups = out_ref.shape[0]
-    rows = 2 * BINS // 3
+    rows = 2 * BINS // 6
     live = live_ref[...].astype(F32)
     live = jnp.concatenate([live, live], axis=1)
     left = lax.broadcasted_iota(jnp.int32, (NB, LANES), 1) < LANES // 2
@@ -254,7 +254,7 @@
         where = pl.ds(pl.multiple_of(begin + step * 8, 8), 8)
         return pltpu.make_async_copy(held.at[step], out_ref.at[:, :, where], sent.at[step])
 
-    @pl.loop(0, steps)
+    @pl.loop(0, steps, unroll=2)
     def _(step):
         base = begin + step * bins
         after_all = next_ref[:, :, pl.ds(pl.multiple_of(step * bins, bins), bins)]

time: 91 us -> 90.7 us (level)
  no operation moved by 1% of the time
where the time goes in v7:
time: 90.7 us; the launch traced here: 90.5 us
  blocking collectives  65.8 us (73%)
  Pallas kernels  16.9 us (19%)
  starting transfers between devices  5.68 us (6%)
  waiting for transfers between devices  1.87 us (2%)
    all_to_all x2, blocking collectives, exchanged(): flat = lax.all_to_all(flat, axis, split_axis=0, concat_axis=0, tiled=True)  65.8 us
    ppermute x2, starting transfers between devices, body(): lax.ppermute(halves[:, 0, :, low:high], 'fibre', back_one)  5.68 us
    pallas_call x1, Pallas kernels, project(): pl.pallas_call(project_kernel, in_specs=[pl.BlockSpec(memory_space=pltpu....  4.98 us
    pallas_call x1, Pallas kernels, whiten(): pl.pallas_call(whiten_kernel, in_specs=[resident] * 3, out_specs=resident...  4.13 us
    pallas_call x2, Pallas kernels, next_spectra(): pl.pallas_call(functools.partial(next_kernel, begin), in_specs=[resident]...  4.06 us
    pallas_call x1, Pallas kernels, own_spectra(): pl.pallas_call(own_kernel, in_specs=[resident] * 2, out_specs=[resident]...  3.71 us
    ppermute x2, waiting for transfers between devices, body(): lax.ppermute(halves[:, 0, :, low:high], 'fibre', back_one)  1.87 us
  transfers between devices with their start and end apart: 2, of which 1 were waited for; matrix products, arithmetic and copies ran while one was open for 0% of the time, Pallas kernels for 6%

profile of v7, /device:TPU:1, one launch (start us, length us, event | category | flops | bytes accessed | tf_op | source)
XLA Modules:
  0.0 90.5 jit_solution(3807597014113978728)
XLA Ops:
  0.0 5.0 %project.1 = bf16[16,6,96,128]{3,2,1,0:T(8,128)(2,1)S(1)} custom-call(bf16[192,375]{1,0:T(8,128)(2,1)} %constant.4.clone.down_ref, bf16[6,375,2048]{2,1,0:T(8,128)(2,1)} %records_ref.1), custom_call_target="tpu_custom_call" | custom-call | flops 1769472000 | bytes 11575296 | tf_op jit(solution)/shard_map/project/pallas_call | solution.py:77
  5.0 0.0 copy-start.1
  5.0 0.0 copy-start.2
  5.0 36.8 %all_to_all.10 = bf16[16,576,128]{2,1,0:T(8,128)(2,1)S(1)} all-to-all(bf16[16,576,128]{2,1,0:T(8,128)(2,1)S(1)} %bitcast.16), channel_id=1, replica_groups=mesh['fibre'=16,'freq'=8] {'fibre'}, dimensions={0} | all-to-all | bytes 4718592 | tf_op jit(solution)/shard_map/all_to_all | solution.py:346
  41.8 0.0 copy-done.1
  41.8 0.0 copy-done.2
  41.8 4.1 %whiten.1 = bf16[8,2,6,64,128]{4,3,2,1,0:T(8,128)(2,1)S(1)} custom-call(s32[1,128]{1,0:T(1,128)S(1)} %bitcast.22, bf16[1152,1536]{1,0:T(8,128)(2,1)S(1)} %copy-done.2, bf16[16,6,96,128]{3,2,1,0:T(8,128)(2,1)S(1)} %bitcast.17), custom_call_target="tpu_custom_call" | custom-call | flops 2717908992 | bytes 7471104 | tf_op jit(solution)/shard_map/whiten/pallas_call | solution.py:147
  45.9 0.0 copy-start
  45.9 29.1 %all_to_all.11 = bf16[8,768,128]{2,1,0:T(8,128)(2,1)S(1)} all-to-all(bf16[8,768,128]{2,1,0:T(8,128)(2,1)S(1)} %bitcast.18), channel_id=1, replica_groups=mesh['fibre'=16,'freq'=8] {'freq'}, dimensions={0} | all-to-all | bytes 3145728 | tf_op jit(solution)/shard_map/all_to_all | solution.py:346
  75.0 0.1 slice_bitcast_fusion
  75.1 3.8 %collective-permute-start.1 = (bf16[8,6,32,128]{3,2,1,0:T(8,128)(2,1)S(1)}, bf16[8,6,32,128]{3,2,1,0:T(8,128)(2,1)S(1)}, u32[]{:S(2)}, u32[]{:S(2)}) collective-permute-start(bf16[8,6,32,128]{3,2,1,0:T(8,128)(2,1)S(1)} %get-tuple-element.9), channel_id=1, source_target_pairs={{8,0},{16,8},{24,16},{32,24},{40,32},{48,40},{56,48},{64,56},{72,6... | collective-permute-start | bytes 1179656 | tf_op jit(solution)/shard_map/ppermute | solution.py:360
  78.9 1.9 %collective-permute-start = (bf16[8,6,32,128]{3,2,1,0:T(8,128)(2,1)S(1)}, bf16[8,6,32,128]{3,2,1,0:T(8,128)(2,1)S(1)}, u32[]{:S(2)}, u32[]{:S(2)}) collective-permute-start(bf16[8,6,32,128]{3,2,1,0:T(8,128)(2,1)S(1)} %get-tuple-element.10), channel_id=1, source_target_pairs={{8,0},{16,8},{24,16},{32,24},{40,32},{48,40},{56,48},{64,56},{72,6... | collective-permute-start | bytes 1179656 | tf_op jit(solution)/shard_map/ppermute | solution.py:360
  80.8 0.0 copy-done
  80.8 3.7 %own_spectra.1 = (f32[64,2,64,128]{3,2,1,0:T(8,128)S(1)}, bf16[64,96,128]{2,1,0:T(8,128)(2,1)S(1)}) custom-call(s32[1,128]{1,0:T(1,128)S(1)} %bitcast.19, bf16[8,2,6,64,128]{4,3,2,1,0:T(8,128)(2,1)S(1)} %bitcast.15), custom_call_target="tpu_custom_call" | custom-call | flops 402653184 | bytes 7340032 | tf_op jit(solution)/shard_map/own_spectra/pallas_call | solution.py:297
  84.5 0.0 collective-permute-done.1.next_ref
  84.5 2.0 %next_spectra.2.refs_0_ = f32[64,2,64,128]{3,2,1,0:T(8,128)} custom-call(s32[1,128]{1,0:T(1,128)S(1)} %bitcast.20, f32[64,2,64,128]{3,2,1,0:T(8,128)S(1)} %get-tuple-element.7.part_ref, bf16[64,96,128]{2,1,0:T(8,128)(2,1)S(1)} %get-tuple-element.8.later_ref, bf16[8,6,32,128]{3,2,1,0:T(8,128)(2,1)S(1)} %collective-permute-done.1.next_ref), custom_call_target="tpu_custom_call" | custom-call | flops 50331648 | bytes 4587520 | tf_op jit(solution)/shard_map/next_spectra/pallas_call | solution.py:323
  86.6 1.9 %collective-permute-done.next_ref = bf16[8,6,32,128]{3,2,1,0:T(8,128)(2,1)S(1)} collective-permute-done((bf16[8,6,32,128]{3,2,1,0:T(8,128)(2,1)S(1)}, bf16[8,6,32,128]{3,2,1,0:T(8,128)(2,1)S(1)}, u32[]{:S(2)}, u32[]{:S(2)}) %collective-permute-start) | collective-permute-done | bytes 393248 | tf_op jit(solution)/shard_map/ppermute | solution.py:360
  88.5 2.0 %next_spectra.3 = f32[64,2,64,128]{3,2,1,0:T(8,128)} custom-call(s32[1,128]{1,0:T(1,128)S(1)} %bitcast.21, f32[64,2,64,128]{3,2,1,0:T(8,128)S(1)} %get-tuple-element.7.part_ref, bf16[64,96,128]{2,1,0:T(8,128)(2,1)S(1)} %get-tuple-element.8.later_ref, bf16[8,6,32,128]{3,2,1,0:T(8,128)(2,1)S(1)} %collective-permute-done.next_ref, ...), custom_call_target="tpu_custom_call", output_to_operand_aliasing={{}: (4, {})} | custom-call | flops 50331648 | bytes 4587520 | tf_op jit(solution)/shard_map/next_spectra/pallas_call | solution.py:323
Async XLA Ops:
  5.0 36.8 %copy-start.1 = (s32[128]{0:T(128)S(1)}, s32[128]{0:T(128)}, u32[]{:S(2)}) copy-start(s32[128]{0:T(128)} %param.6) | copy-start | bytes 1540
  5.0 36.8 %copy-start.2 = (bf16[1152,1536]{1,0:T(8,128)(2,1)S(1)}, bf16[1152,1536]{1,0:T(8,128)(2,1)}, u32[]{:S(2)}) copy-start(bf16[1152,1536]{1,0:T(8,128)(2,1)} %constant.5.clone.back_ref) | copy-start | bytes 10616836
  45.9 34.9 %copy-start = (s32[128]{0:T(128)S(1)}, s32[128]{0:T(128)}, u32[]{:S(2)}) copy-start(s32[128]{0:T(128)} %param.7) | copy-start | bytes 1540
  75.1 9.4 %collective-permute-start.1 = (bf16[8,6,32,128]{3,2,1,0:T(8,128)(2,1)S(1)}, bf16[8,6,32,128]{3,2,1,0:T(8,128)(2,1)S(1)}, u32[]{:S(2)}, u32[]{:S(2)}) collective-permute-start(bf16[8,6,32,128]{3,2,1,0:T(8,128)(2,1)S(1)} %get-tuple-element.9), channel_id=1, source_target_pairs={{8,0},{16,8},{24,16},{32,24},{40,32},{48,40},{56,48},{64,56},{72,6... | collective-permute-start | bytes 1179656 | tf_op jit(solution)/shard_map/ppermute | solution.py:360
  78.9 9.6 %collective-permute-start = (bf16[8,6,32,128]{3,2,1,0:T(8,128)(2,1)S(1)}, bf16[8,6,32,128]{3,2,1,0:T(8,128)(2,1)S(1)}, u32[]{:S(2)}, u32[]{:S(2)}) collective-permute-start(bf16[8,6,32,128]{3,2,1,0:T(8,128)(2,1)S(1)} %get-tuple-element.10), channel_id=1, source_target_pairs={{8,0},{16,8},{24,16},{32,24},{40,32},{48,40},{56,48},{64,56},{72,6... | collective-permute-start | bytes 1179656 | tf_op jit(solution)/shard_map/ppermute | solution.py:360

commit v8 on v7

--- a/solution.py
+++ b/solution.py
@@ -254,7 +254,7 @@
         where = pl.ds(pl.multiple_of(begin + step * 8, 8), 8)
         return pltpu.make_async_copy(held.at[step], out_ref.at[:, :, where], sent.at[step])
 
-    @pl.loop(0, steps, unroll=2)
+    @pl.loop(0, steps, unroll=steps)
     def _(step):
         base = begin + step * bins
         after_all = next_ref[:, :, pl.ds(pl.multiple_of(step * bins, bins), bins)]
@@ -355,7 +355,7 @@
     halves = whiten(channel_live[None, :], back, sums, groups)
     halves = exchanged(halves, "freq")
     back_one = [(i, i - 1) for i in range(1, parts)]
-    bounds = (0, 32, NB // groups)
+    bounds = (0, 48, NB // groups)
     after = [
         lax.ppermute(halves[:, 0, :, low:high], "fibre", back_one)
         for low, high in zip(bounds, bounds[1:])

time: 90.7 us -> 90.7 us (level)
  transfers between devices with their start and end apart: 2 -> 2, of which waited for: 1 -> 1; matrix products, arithmetic and copies ran while one was open for 0% -> 0% of each run, Pallas kernels for 6% -> 7%
where the time goes in v8:
time: 90.7 us; the launch traced here: 90.5 us
  blocking collectives  65.8 us (73%)
  Pallas kernels  17 us (19%)
  starting transfers between devices  5.68 us (6%)
  waiting for transfers between devices  1.78 us (2%)
    all_to_all x2, blocking collectives, exchanged(): flat = lax.all_to_all(flat, axis, split_axis=0, concat_axis=0, tiled=True)  65.8 us
    ppermute x2, starting transfers between devices, body(): lax.ppermute(halves[:, 0, :, low:high], 'fibre', back_one)  5.68 us
    pallas_call x1, Pallas kernels, project(): pl.pallas_call(project_kernel, in_specs=[pl.BlockSpec(memory_space=pltpu....  4.98 us
    pallas_call x2, Pallas kernels, next_spectra(): pl.pallas_call(functools.partial(next_kernel, begin), in_specs=[resident]...  4.15 us
    pallas_call x1, Pallas kernels, whiten(): pl.pallas_call(whiten_kernel, in_specs=[resident] * 3, out_specs=resident...  4.13 us
    pallas_call x1, Pallas kernels, own_spectra(): pl.pallas_call(own_kernel, in_specs=[resident] * 2, out_specs=[resident]...  3.71 us
  transfers between devices with their start and end apart: 2, of which 1 were waited for; matrix products, arithmetic and copies ran while one was open for 0% of the time, Pallas kernels for 7%

profile of v8, /device:TPU:1, one launch (start us, length us, event | category | flops | bytes accessed | tf_op | source)
XLA Modules:
  0.0 90.5 jit_solution(1258288164663652645)
XLA Ops:
  0.0 5.0 %project.1 = bf16[16,6,96,128]{3,2,1,0:T(8,128)(2,1)S(1)} custom-call(bf16[192,375]{1,0:T(8,128)(2,1)} %constant.4.clone.down_ref, bf16[6,375,2048]{2,1,0:T(8,128)(2,1)} %records_ref.1), custom_call_target="tpu_custom_call" | custom-call | flops 1769472000 | bytes 11575296 | tf_op jit(solution)/shard_map/project/pallas_call | solution.py:77
  5.0 0.0 copy-start.1
  5.0 0.0 copy-start.2
  5.0 36.8 %all_to_all.10 = bf16[16,576,128]{2,1,0:T(8,128)(2,1)S(1)} all-to-all(bf16[16,576,128]{2,1,0:T(8,128)(2,1)S(1)} %bitcast.17), channel_id=1, replica_groups=mesh['fibre'=16,'freq'=8] {'fibre'}, dimensions={0} | all-to-all | bytes 4718592 | tf_op jit(solution)/shard_map/all_to_all | solution.py:346
  41.8 0.0 copy-done.1
  41.8 0.0 copy-done.2
  41.8 4.1 %whiten.1 = bf16[8,2,6,64,128]{4,3,2,1,0:T(8,128)(2,1)S(1)} custom-call(s32[1,128]{1,0:T(1,128)S(1)} %bitcast.23, bf16[1152,1536]{1,0:T(8,128)(2,1)S(1)} %copy-done.2, bf16[16,6,96,128]{3,2,1,0:T(8,128)(2,1)S(1)} %bitcast.18), custom_call_target="tpu_custom_call" | custom-call | flops 2717908992 | bytes 7471104 | tf_op jit(solution)/shard_map/whiten/pallas_call | solution.py:147
  45.9 0.0 copy-start
  45.9 29.1 %all_to_all.11 = bf16[8,768,128]{2,1,0:T(8,128)(2,1)S(1)} all-to-all(bf16[8,768,128]{2,1,0:T(8,128)(2,1)S(1)} %bitcast.19), channel_id=1, replica_groups=mesh['fibre'=16,'freq'=8] {'freq'}, dimensions={0} | all-to-all | bytes 3145728 | tf_op jit(solution)/shard_map/all_to_all | solution.py:346
  75.0 0.1 slice_bitcast_fusion
  75.1 3.8 %collective-permute-start.1 = (bf16[8,6,48,128]{3,2,1,0:T(8,128)(2,1)S(1)}, bf16[8,6,48,128]{3,2,1,0:T(8,128)(2,1)S(1)}, u32[]{:S(2)}, u32[]{:S(2)}) collective-permute-start(bf16[8,6,48,128]{3,2,1,0:T(8,128)(2,1)S(1)} %slice_bitcast_fusion), channel_id=1, source_target_pairs={{8,0},{16,8},{24,16},{32,24},{40,32},{48,40},{56,48},{64,56},{72,6... | collective-permute-start | bytes 1769480 | tf_op jit(solution)/shard_map/ppermute | solution.py:360
  78.9 1.9 %collective-permute-start = (bf16[8,6,16,128]{3,2,1,0:T(8,128)(2,1)S(1)}, bf16[8,6,16,128]{3,2,1,0:T(8,128)(2,1)S(1)}, u32[]{:S(2)}, u32[]{:S(2)}) collective-permute-start(bf16[8,6,16,128]{3,2,1,0:T(8,128)(2,1)S(1)} %slice_bitcast_fusion.1), channel_id=1, source_target_pairs={{8,0},{16,8},{24,16},{32,24},{40,32},{48,40},{56,48},{64,56},{72,6... | collective-permute-start | bytes 589832 | tf_op jit(solution)/shard_map/ppermute | solution.py:360
  80.8 0.0 copy-done
  80.8 3.7 %own_spectra.1 = (f32[64,2,64,128]{3,2,1,0:T(8,128)S(1)}, bf16[64,96,128]{2,1,0:T(8,128)(2,1)S(1)}) custom-call(s32[1,128]{1,0:T(1,128)S(1)} %bitcast.20, bf16[8,2,6,64,128]{4,3,2,1,0:T(8,128)(2,1)S(1)} %bitcast.16), custom_call_target="tpu_custom_call" | custom-call | flops 402653184 | bytes 7340032 | tf_op jit(solution)/shard_map/own_spectra/pallas_call | solution.py:297
  84.5 1.8 %collective-permute-done.1.next_ref = bf16[8,6,48,128]{3,2,1,0:T(8,128)(2,1)S(1)} collective-permute-done((bf16[8,6,48,128]{3,2,1,0:T(8,128)(2,1)S(1)}, bf16[8,6,48,128]{3,2,1,0:T(8,128)(2,1)S(1)}, u32[]{:S(2)}, u32[]{:S(2)}) %collective-permute-start.1) | collective-permute-done | bytes 589856 | tf_op jit(solution)/shard_map/ppermute | solution.py:360
  86.3 2.6 %next_spectra.2.refs_0_ = f32[64,2,64,128]{3,2,1,0:T(8,128)} custom-call(s32[1,128]{1,0:T(1,128)S(1)} %bitcast.21, f32[64,2,64,128]{3,2,1,0:T(8,128)S(1)} %get-tuple-element.7.part_ref, bf16[64,96,128]{2,1,0:T(8,128)(2,1)S(1)} %get-tuple-element.8.later_ref, bf16[8,6,48,128]{3,2,1,0:T(8,128)(2,1)S(1)} %collective-permute-done.1.next_ref), custom_call_target="tpu_custom_call" | custom-call | flops 75497472 | bytes 6881280 | tf_op jit(solution)/shard_map/next_spectra/pallas_call | solution.py:323
  89.0 0.0 collective-permute-done.next_ref
  89.0 1.5 %next_spectra.3 = f32[64,2,64,128]{3,2,1,0:T(8,128)} custom-call(s32[1,128]{1,0:T(1,128)S(1)} %bitcast.22, f32[64,2,64,128]{3,2,1,0:T(8,128)S(1)} %get-tuple-element.7.part_ref, bf16[64,96,128]{2,1,0:T(8,128)(2,1)S(1)} %get-tuple-element.8.later_ref, bf16[8,6,16,128]{3,2,1,0:T(8,128)(2,1)S(1)} %collective-permute-done.next_ref, ...), custom_call_target="tpu_custom_call", output_to_operand_aliasing={{}: (4, {})} | custom-call | flops 25165824 | bytes 2293760 | tf_op jit(solution)/shard_map/next_spectra/pallas_call | solution.py:323
  (1 shorter events, 0.0 us)
Async XLA Ops:
  5.0 36.8 %copy-start.1 = (s32[128]{0:T(128)S(1)}, s32[128]{0:T(128)}, u32[]{:S(2)}) copy-start(s32[128]{0:T(128)} %param.6) | copy-start | bytes 1540
  5.0 36.8 %copy-start.2 = (bf16[1152,1536]{1,0:T(8,128)(2,1)S(1)}, bf16[1152,1536]{1,0:T(8,128)(2,1)}, u32[]{:S(2)}) copy-start(bf16[1152,1536]{1,0:T(8,128)(2,1)} %constant.5.clone.back_ref) | copy-start | bytes 10616836
  45.9 34.9 %copy-start = (s32[128]{0:T(128)S(1)}, s32[128]{0:T(128)}, u32[]{:S(2)}) copy-start(s32[128]{0:T(128)} %param.7) | copy-start | bytes 1540
  75.1 11.2 %collective-permute-start.1 = (bf16[8,6,48,128]{3,2,1,0:T(8,128)(2,1)S(1)}, bf16[8,6,48,128]{3,2,1,0:T(8,128)(2,1)S(1)}, u32[]{:S(2)}, u32[]{:S(2)}) collective-permute-start(bf16[8,6,48,128]{3,2,1,0:T(8,128)(2,1)S(1)} %slice_bitcast_fusion), channel_id=1, source_target_pairs={{8,0},{16,8},{24,16},{32,24},{40,32},{48,40},{56,48},{64,56},{72,6... | collective-permute-start | bytes 1769480 | tf_op jit(solution)/shard_map/ppermute | solution.py:360
  78.9 10.1 %collective-permute-start = (bf16[8,6,16,128]{3,2,1,0:T(8,128)(2,1)S(1)}, bf16[8,6,16,128]{3,2,1,0:T(8,128)(2,1)S(1)}, u32[]{:S(2)}, u32[]{:S(2)}) collective-permute-start(bf16[8,6,16,128]{3,2,1,0:T(8,128)(2,1)S(1)} %slice_bitcast_fusion.1), channel_id=1, source_target_pairs={{8,0},{16,8},{24,16},{32,24},{40,32},{48,40},{56,48},{64,56},{72,6... | collective-permute-start | bytes 589832 | tf_op jit(solution)/shard_map/ppermute | solution.py:360

commit v9 on v7

--- a/solution.py
+++ b/solution.py
@@ -250,9 +250,11 @@
     lanes = lax.broadcasted_iota(jnp.int32, (OFFSETS, LANES), 1)
     keep = ((offsets <= limit_ref[...]) & (lanes >= half)).astype(F32)
 
-    def send(step):
+    def send(step, part):
         where = pl.ds(pl.multiple_of(begin + step * 8, 8), 8)
-        return pltpu.make_async_copy(held.at[step], out_ref.at[:, :, where], sent.at[step])
+        return pltpu.make_async_copy(
+            held.at[step, part], out_ref.at[:, part, where], sent.at[step, part]
+        )
 
     @pl.loop(0, steps, unroll=2)
     def _(step):
@@ -283,11 +285,12 @@
                         own = part_ref[base + start + at, part, tile : tile + 8]
                         sums.append(own + value)
                     for at, value in enumerate(swapped(sums)):
-                        held[2 * step + start // 8, tile + at, part] = value
-            send(2 * step + start // 8).start()
+                        held[2 * step + start // 8, part, tile + at] = value
+                send(2 * step + start // 8, part).start()
 
     for step in range(2 * steps):
-        send(step).wait()
+        for part in range(2):
+            send(step, part).wait()
 
 
 def own_spectra(limit, halves):
@@ -328,8 +331,8 @@
         input_output_aliases={4: 0} if filled else {},
         scratch_shapes=[
             pltpu.VMEM(((every + 1) * PITCH, LANES), F32),
-            pltpu.VMEM((bins // 8, OFFSETS, 2, 8, LANES), F32),
-            pltpu.SemaphoreType.DMA((bins // 8,)),
+            pltpu.VMEM((bins // 8, 2, OFFSETS, 8, LANES), F32),
+            pltpu.SemaphoreType.DMA((bins // 8, 2)),
         ],
         compiler_params=pltpu.CompilerParams(vmem_limit_bytes=20 * 2**20),
         cost_estimate=pl.CostEstimate(

time: 90.7 us -> 90.7 us (level)
  no operation moved by 1% of the time
where the time goes in v9:
time: 90.7 us; the launch traced here: 90.5 us
  blocking collectives  65.8 us (73%)
  Pallas kernels  17 us (19%)
  starting transfers between devices  5.68 us (6%)
  waiting for transfers between devices  1.82 us (2%)
    all_to_all x2, blocking collectives, exchanged(): flat = lax.all_to_all(flat, axis, split_axis=0, concat_axis=0, tiled=True)  65.8 us
    ppermute x2, starting transfers between devices, body(): lax.ppermute(halves[:, 0, :, low:high], 'fibre', back_one)  5.68 us
    pallas_call x1, Pallas kernels, project(): pl.pallas_call(project_kernel, in_specs=[pl.BlockSpec(memory_space=pltpu....  4.98 us
    pallas_call x2, Pallas kernels, next_spectra(): pl.pallas_call(functools.partial(next_kernel, begin), in_specs=[resident]...  4.17 us
    pallas_call x1, Pallas kernels, whiten(): pl.pallas_call(whiten_kernel, in_specs=[resident] * 3, out_specs=resident...  4.13 us
    pallas_call x1, Pallas kernels, own_spectra(): pl.pallas_call(own_kernel, in_specs=[resident] * 2, out_specs=[resident]...  3.71 us
    ppermute x2, waiting for transfers between devices, body(): lax.ppermute(halves[:, 0, :, low:high], 'fibre', back_one)  1.82 us
  transfers between devices with their start and end apart: 2, of which 1 were waited for; matrix products, arithmetic and copies ran while one was open for 0% of the time, Pallas kernels for 6%

profile of v9, /device:TPU:1, one launch (start us, length us, event | category | flops | bytes accessed | tf_op | source)
XLA Modules:
  0.0 90.5 jit_solution(7089085391914898631)
XLA Ops:
  0.0 5.0 %project.1 = bf16[16,6,96,128]{3,2,1,0:T(8,128)(2,1)S(1)} custom-call(bf16[192,375]{1,0:T(8,128)(2,1)} %constant.4.clone.down_ref, bf16[6,375,2048]{2,1,0:T(8,128)(2,1)} %records_ref.1), custom_call_target="tpu_custom_call" | custom-call | flops 1769472000 | bytes 11575296 | tf_op jit(solution)/shard_map/project/pallas_call | solution.py:77
  5.0 0.0 copy-start.1
  5.0 0.0 copy-start.2
  5.0 36.8 %all_to_all.10 = bf16[16,576,128]{2,1,0:T(8,128)(2,1)S(1)} all-to-all(bf16[16,576,128]{2,1,0:T(8,128)(2,1)S(1)} %bitcast.16), channel_id=1, replica_groups=mesh['fibre'=16,'freq'=8] {'fibre'}, dimensions={0} | all-to-all | bytes 4718592 | tf_op jit(solution)/shard_map/all_to_all | solution.py:349
  41.8 0.0 copy-done.1
  41.8 0.0 copy-done.2
  41.8 4.1 %whiten.1 = bf16[8,2,6,64,128]{4,3,2,1,0:T(8,128)(2,1)S(1)} custom-call(s32[1,128]{1,0:T(1,128)S(1)} %bitcast.22, bf16[1152,1536]{1,0:T(8,128)(2,1)S(1)} %copy-done.2, bf16[16,6,96,128]{3,2,1,0:T(8,128)(2,1)S(1)} %bitcast.17), custom_call_target="tpu_custom_call" | custom-call | flops 2717908992 | bytes 7471104 | tf_op jit(solution)/shard_map/whiten/pallas_call | solution.py:147
  45.9 0.0 copy-start
  45.9 29.1 %all_to_all.11 = bf16[8,768,128]{2,1,0:T(8,128)(2,1)S(1)} all-to-all(bf16[8,768,128]{2,1,0:T(8,128)(2,1)S(1)} %bitcast.18), channel_id=1, replica_groups=mesh['fibre'=16,'freq'=8] {'freq'}, dimensions={0} | all-to-all | bytes 3145728 | tf_op jit(solution)/shard_map/all_to_all | solution.py:349
  75.0 0.1 slice_bitcast_fusion
  75.1 3.8 %collective-permute-start.1 = (bf16[8,6,32,128]{3,2,1,0:T(8,128)(2,1)S(1)}, bf16[8,6,32,128]{3,2,1,0:T(8,128)(2,1)S(1)}, u32[]{:S(2)}, u32[]{:S(2)}) collective-permute-start(bf16[8,6,32,128]{3,2,1,0:T(8,128)(2,1)S(1)} %get-tuple-element.9), channel_id=1, source_target_pairs={{8,0},{16,8},{24,16},{32,24},{40,32},{48,40},{56,48},{64,56},{72,6... | collective-permute-start | bytes 1179656 | tf_op jit(solution)/shard_map/ppermute | solution.py:363
  78.9 1.9 %collective-permute-start = (bf16[8,6,32,128]{3,2,1,0:T(8,128)(2,1)S(1)}, bf16[8,6,32,128]{3,2,1,0:T(8,128)(2,1)S(1)}, u32[]{:S(2)}, u32[]{:S(2)}) collective-permute-start(bf16[8,6,32,128]{3,2,1,0:T(8,128)(2,1)S(1)} %get-tuple-element.10), channel_id=1, source_target_pairs={{8,0},{16,8},{24,16},{32,24},{40,32},{48,40},{56,48},{64,56},{72,6... | collective-permute-start | bytes 1179656 | tf_op jit(solution)/shard_map/ppermute | solution.py:363
  80.8 0.0 copy-done
  80.8 3.7 %own_spectra.1 = (f32[64,2,64,128]{3,2,1,0:T(8,128)S(1)}, bf16[64,96,128]{2,1,0:T(8,128)(2,1)S(1)}) custom-call(s32[1,128]{1,0:T(1,128)S(1)} %bitcast.19, bf16[8,2,6,64,128]{4,3,2,1,0:T(8,128)(2,1)S(1)} %bitcast.15), custom_call_target="tpu_custom_call" | custom-call | flops 402653184 | bytes 7340032 | tf_op jit(solution)/shard_map/own_spectra/pallas_call | solution.py:300
  84.5 0.0 collective-permute-done.1.next_ref
  84.5 2.1 %next_spectra.2.refs_0_ = f32[64,2,64,128]{3,2,1,0:T(8,128)} custom-call(s32[1,128]{1,0:T(1,128)S(1)} %bitcast.20, f32[64,2,64,128]{3,2,1,0:T(8,128)S(1)} %get-tuple-element.7.part_ref, bf16[64,96,128]{2,1,0:T(8,128)(2,1)S(1)} %get-tuple-element.8.later_ref, bf16[8,6,32,128]{3,2,1,0:T(8,128)(2,1)S(1)} %collective-permute-done.1.next_ref), custom_call_target="tpu_custom_call" | custom-call | flops 50331648 | bytes 4587520 | tf_op jit(solution)/shard_map/next_spectra/pallas_call | solution.py:326
  86.6 1.8 %collective-permute-done.next_ref = bf16[8,6,32,128]{3,2,1,0:T(8,128)(2,1)S(1)} collective-permute-done((bf16[8,6,32,128]{3,2,1,0:T(8,128)(2,1)S(1)}, bf16[8,6,32,128]{3,2,1,0:T(8,128)(2,1)S(1)}, u32[]{:S(2)}, u32[]{:S(2)}) %collective-permute-start) | collective-permute-done | bytes 393248 | tf_op jit(solution)/shard_map/ppermute | solution.py:363
  88.5 2.1 %next_spectra.3 = f32[64,2,64,128]{3,2,1,0:T(8,128)} custom-call(s32[1,128]{1,0:T(1,128)S(1)} %bitcast.21, f32[64,2,64,128]{3,2,1,0:T(8,128)S(1)} %get-tuple-element.7.part_ref, bf16[64,96,128]{2,1,0:T(8,128)(2,1)S(1)} %get-tuple-element.8.later_ref, bf16[8,6,32,128]{3,2,1,0:T(8,128)(2,1)S(1)} %collective-permute-done.next_ref, ...), custom_call_target="tpu_custom_call", output_to_operand_aliasing={{}: (4, {})} | custom-call | flops 50331648 | bytes 4587520 | tf_op jit(solution)/shard_map/next_spectra/pallas_call | solution.py:326
Async XLA Ops:
  5.0 36.8 %copy-start.1 = (s32[128]{0:T(128)S(1)}, s32[128]{0:T(128)}, u32[]{:S(2)}) copy-start(s32[128]{0:T(128)} %param.6) | copy-start | bytes 1540
  5.0 36.8 %copy-start.2 = (bf16[1152,1536]{1,0:T(8,128)(2,1)S(1)}, bf16[1152,1536]{1,0:T(8,128)(2,1)}, u32[]{:S(2)}) copy-start(bf16[1152,1536]{1,0:T(8,128)(2,1)} %constant.5.clone.back_ref) | copy-start | bytes 10616836
  45.9 34.9 %copy-start = (s32[128]{0:T(128)S(1)}, s32[128]{0:T(128)}, u32[]{:S(2)}) copy-start(s32[128]{0:T(128)} %param.7) | copy-start | bytes 1540
  75.1 9.4 %collective-permute-start.1 = (bf16[8,6,32,128]{3,2,1,0:T(8,128)(2,1)S(1)}, bf16[8,6,32,128]{3,2,1,0:T(8,128)(2,1)S(1)}, u32[]{:S(2)}, u32[]{:S(2)}) collective-permute-start(bf16[8,6,32,128]{3,2,1,0:T(8,128)(2,1)S(1)} %get-tuple-element.9), channel_id=1, source_target_pairs={{8,0},{16,8},{24,16},{32,24},{40,32},{48,40},{56,48},{64,56},{72,6... | collective-permute-start | bytes 1179656 | tf_op jit(solution)/shard_map/ppermute | solution.py:363
  78.9 9.6 %collective-permute-start = (bf16[8,6,32,128]{3,2,1,0:T(8,128)(2,1)S(1)}, bf16[8,6,32,128]{3,2,1,0:T(8,128)(2,1)S(1)}, u32[]{:S(2)}, u32[]{:S(2)}) collective-permute-start(bf16[8,6,32,128]{3,2,1,0:T(8,128)(2,1)S(1)} %get-tuple-element.10), channel_id=1, source_target_pairs={{8,0},{16,8},{24,16},{32,24},{40,32},{48,40},{56,48},{64,56},{72,6... | collective-permute-start | bytes 1179656 | tf_op jit(solution)/shard_map/ppermute | solution.py:363
